TPU v7x, 256 devices: a whole 4x4x8 slice. The times are simulated.
256 devices in a mesh: blk: 128 (over x, y_hi, z, core), rep: 2 (over y_lo).
Axes of the slice: x: 4, y: 4 (y_hi: 2, y_lo: 2; y = y_hi * 2 + y_lo), z: 8, core: 2. Of those that a mesh axis runs over, the one named last changes fastest.
Arguments:
- embeddings: bfloat16 [131072, 768], P('blk', 'rep'), as said below
- weights: bfloat16 [131072], P('blk'), may hold values from 0.25 to 4
Outputs:
- neighbours: bfloat16 [131072, 768], P('blk', 'rep')
- scores: float32 [131072], P('blk')
Inputs may be any that keep to these rules, and one draw needn't show every extreme that they name: `embeddings`: finite values.
All inputs are finite; a program needn't handle non-finite values.
Results may differ from a plain program's by a relative error of at most 0.0034.
Values may be sent and summed in bfloat16 or wider, within the bound.
No kernel may reach another device: no remote copies, remote signals or barrier semaphores. Data moves between devices by JAX's collectives and lax.ppermute only.
A program may use at most 64 MiB of HBM per device.

v0:
```python
import jax
import jax.numpy as jnp
from jax import lax
from jax.sharding import PartitionSpec as P

sharpness = 12.0
epsilon = 1e-06


def passed_along(value, axis, steps):
    count = lax.axis_size(axis)
    pairs = [(source, (source + steps) % count) for source in range(count)]
    return lax.ppermute(value, axis, pairs)


def prepare(embeddings, weights):
    values = embeddings.astype(jnp.float32)
    root_mean = jnp.sqrt(jnp.mean(values * values, axis=1, keepdims=True) + epsilon)
    scaled = values / root_mean
    unit_rows = scaled.astype(jnp.bfloat16)
    value_rows = (weights.astype(jnp.float32)[:, None] * scaled).astype(jnp.bfloat16)
    return (unit_rows, value_rows)


def kernel_of(queries, keys_unit):
    cosine = lax.dot_general(
        queries, keys_unit, (((1,), (1,)), ((), ())), preferred_element_type=jnp.float32
    )
    cosine = cosine / queries.shape[1]
    return jnp.exp(sharpness * (cosine - 1.0))


def tile_terms(unit_rows, query_values, weights, moving):
    kernel = kernel_of(unit_rows, moving[0]).astype(jnp.bfloat16)
    row_part = jnp.dot(kernel, moving[1], preferred_element_type=jnp.float32)
    mass_part = jnp.dot(kernel, moving[2], preferred_element_type=jnp.float32)
    column_sums = lax.dot_general(
        kernel, query_values, (((0,), (0,)), ((), ())), preferred_element_type=jnp.float32
    )
    column_mass = jnp.dot(weights, kernel, preferred_element_type=jnp.float32)
    return (row_part, mass_part, (column_sums, column_mass))


def shards(embeddings, weights):
    groups = lax.axis_size("rep")
    rep_index = lax.axis_index("rep")
    gathered = lax.all_gather(embeddings, "rep", axis=1, tiled=True)
    unit_rows, value_rows = prepare(gathered, weights)
    rows_all = gathered.shape[0]
    half_rows = rows_all // groups
    start = rep_index * half_rows
    returned = []
    own_unit = lax.dynamic_slice_in_dim(unit_rows, start, half_rows, 0)
    own_value = lax.dynamic_slice_in_dim(value_rows, start, half_rows, 0)
    own_weight = lax.dynamic_slice_in_dim(weights, start, half_rows, 0)
    kernel = kernel_of(unit_rows, own_unit)
    row_ids = jnp.arange(rows_all, dtype=jnp.int32)[:, None]
    col_ids = start + jnp.arange(half_rows, dtype=jnp.int32)[None, :]
    kernel = jnp.where(row_ids == col_ids, jnp.zeros_like(kernel), kernel).astype(jnp.bfloat16)
    row_sums = jnp.dot(kernel, own_value, preferred_element_type=jnp.float32)
    masses = jnp.dot(kernel, own_weight, preferred_element_type=jnp.float32)
    moving = (own_unit, own_value, own_weight)
    for offset in range(2):
        moving = passed_along((moving[0], moving[1], moving[2]), "blk", -1)
        row_part, mass_part, back = tile_terms(unit_rows, value_rows, weights, moving)
        row_sums = row_sums + row_part
        masses = masses + mass_part
        returned.append(back)
    back_sums = jnp.zeros(returned[0][0].shape, jnp.float32)
    back_mass = jnp.zeros(returned[0][1].shape, jnp.float32)
    for offset in range(2):
        arrived = passed_along(returned[offset], "blk", offset + 1)
        back_sums = back_sums + arrived[0]
        back_mass = back_mass + arrived[1]
    own_sums = lax.dynamic_slice_in_dim(row_sums, start, half_rows, 0) + back_sums
    row_sums = lax.dynamic_update_slice_in_dim(row_sums, own_sums, start, 0)
    own_mass = lax.dynamic_slice_in_dim(masses, start, half_rows, 0) + back_mass
    masses = lax.dynamic_update_slice_in_dim(masses, own_mass, start, 0)
    feature_sums = lax.psum_scatter(row_sums, "rep", scatter_dimension=1, tiled=True)
    total_mass = lax.psum(masses, "rep")
    neighbours = (feature_sums / total_mass[:, None]).astype(jnp.bfloat16)
    scores = jnp.log(total_mass) / sharpness + 1.0
    return (neighbours, scores)


def solution(mesh):
    return jax.shard_map(
        shards,
        mesh=mesh,
        in_specs=(P("blk", "rep"), P("blk")),
        out_specs=(P("blk", "rep"), P("blk")),
        check_vma=False,
    )
```

profile of v0, /device:TPU:1, one launch (start us, length us, event | category | flops | bytes accessed | tf_op | source)
XLA Modules:
  0.0 185.0 jit_solution(12404976071092412597)
XLA Ops:
  7.2 0.7 all-gather.2.cloned.1.call-update
  7.9 0.7 convert_element_type.27
  8.6 37.3 %all-gather.2.cloned.1.call-done = bf16[1024,768]{1,0:T(8,128)(2,1)} async-done(((bf16[1024,384]{1,0:T(8,128)(2,1)}), bf16[1024,768]{1,0:T(8,128)(2,1)}) %all-gather.2.cloned.1.call-update) | async-done | bytes 1572880 | tf_op jit(solution)/shard_map/all_gather | solution.py:47
  45.9 1.9 %fusion = f32[1024]{0:T(1024)S(1)} fusion(bf16[1024,768]{1,0:T(8,128)(2,1)} %all-gather.2.cloned.1.call-done), kind=kLoop, calls=%fused_computation.2 | loop fusion | flops 2358272 | bytes 1576960 | tf_op jit(solution)/shard_map/reduce_sum | solution.py:18
  48.5 0.8 collective-permute-start
  49.3 7.1 %collective-permute-start.1 = (bf16[512,768]{1,0:T(8,128)(2,1)S(1)}, bf16[512,768]{1,0:T(8,128)(2,1)S(1)}, u32[]{:S(2)}, u32[]{:S(2)}) collective-permute-start(bf16[512,768]{1,0:T(8,128)(2,1)S(1)} %constant_dynamic-slice_fusion), channel_id=1, source_target_pairs={{0,254},{2,0},{4,2},{6,4},{8,6},{10,8},{12,10},{14,12},{16,14},{18... | collective-permute-start | bytes 2359304 | tf_op jit(solution)/shard_map/ppermute | solution.py:13
  56.4 3.7 %collective-permute-done = bf16[512,768]{1,0:T(8,128)(2,1)S(1)} collective-permute-done((bf16[512,768]{1,0:T(8,128)(2,1)S(1)}, bf16[512,768]{1,0:T(8,128)(2,1)S(1)}, u32[]{:S(2)}, u32[]{:S(2)}) %collective-permute-start) | collective-permute-done | bytes 786464 | tf_op jit(solution)/shard_map/ppermute | solution.py:13
  60.1 5.7 %collective-permute-start.2 = (bf16[512,768]{1,0:T(8,128)(2,1)S(1)}, bf16[512,768]{1,0:T(8,128)(2,1)S(1)}, u32[]{:S(2)}, u32[]{:S(2)}) collective-permute-start(bf16[512,768]{1,0:T(8,128)(2,1)S(1)} %collective-permute-done), channel_id=1, source_target_pairs={{0,254},{2,0},{4,2},{6,4},{8,6},{10,8},{12,10},{14,12},{16,14},{18... | collective-permute-start | bytes 2359304 | tf_op jit(solution)/shard_map/ppermute | solution.py:13
  65.8 1.1 exponential_convert_fusion.1
  66.9 1.0 fusion.4
  68.5 7.3 %collective-permute-start.3 = (bf16[512,768]{1,0:T(8,128)(2,1)S(1)}, bf16[512,768]{1,0:T(8,128)(2,1)S(1)}, u32[]{:S(2)}, u32[]{:S(2)}) collective-permute-start(bf16[512,768]{1,0:T(8,128)(2,1)S(1)} %collective-permute-done.1), channel_id=1, source_target_pairs={{0,254},{2,0},{4,2},{6,4},{8,6},{10,8},{12,10},{14,12},{16,14},{18... | collective-permute-start | bytes 2359304 | tf_op jit(solution)/shard_map/ppermute | solution.py:13
  75.8 1.1 collective-permute-done.2
  76.9 1.1 exponential_convert_fusion
  78.1 1.0 fusion.5
  79.1 1.8 collective-permute-start.5
  80.9 1.3 select_convert_fusion
  82.2 1.0 fusion.2
  83.2 1.0 fusion.3
  84.2 1.4 collective-permute-done.3
  85.6 1.0 add_add_fusion
  86.6 47.6 %collective-permute-done.5 = f32[512,768]{1,0:T(8,128)S(1)} collective-permute-done((f32[512,768]{1,0:T(8,128)S(1)}, f32[512,768]{1,0:T(8,128)S(1)}, u32[]{:S(2)}, u32[]{:S(2)}) %collective-permute-start.5) | collective-permute-done | bytes 1572896 | tf_op jit(solution)/shard_map/ppermute | solution.py:13
  134.8 1.6 copy-done
  136.6 3.0 %collective-permute-done.6 = bf16[512]{0:T(512)(128)(2,1)S(1)} collective-permute-done((bf16[512]{0:T(512)(128)(2,1)S(1)}, bf16[512]{0:T(512)(128)(2,1)S(1)}, u32[]{:S(2)}, u32[]{:S(2)}) %collective-permute-start.6) | collective-permute-done | bytes 1056 | tf_op jit(solution)/shard_map/ppermute | solution.py:13
  139.6 3.4 %collective-permute-done.7 = bf16[512]{0:T(512)(128)(2,1)S(1)} collective-permute-done((bf16[512]{0:T(512)(128)(2,1)S(1)}, bf16[512]{0:T(512)(128)(2,1)S(1)}, u32[]{:S(2)}, u32[]{:S(2)}) %collective-permute-start.7) | collective-permute-done | bytes 1056 | tf_op jit(solution)/shard_map/ppermute | solution.py:13
  142.9 1.6 fusion.6
  144.5 1.5 fusion.9
  147.0 3.2 %collective-permute-done.8 = f32[512]{0:T(512)S(1)} collective-permute-done((f32[512]{0:T(512)S(1)}, f32[512]{0:T(512)S(1)}, u32[]{:S(2)}, u32[]{:S(2)}) %collective-permute-start.8) | collective-permute-done | bytes 2080 | tf_op jit(solution)/shard_map/ppermute | solution.py:13
  150.2 8.1 %collective-permute-done.9 = f32[512]{0:T(512)S(1)} collective-permute-done((f32[512]{0:T(512)S(1)}, f32[512]{0:T(512)S(1)}, u32[]{:S(2)}, u32[]{:S(2)}) %collective-permute-start.9) | collective-permute-done | bytes 2080 | tf_op jit(solution)/shard_map/ppermute | solution.py:13
  158.5 4.2 %psum.7 = f32[1024]{0:T(1024)S(1)} all-reduce(f32[1024]{0:T(1024)S(1)} %add_dynamic-update-slice_fusion.1), channel_id=1, replica_groups=mesh['blk'=128,'rep'=2] {'rep'}, use_global_device_ids=true, to_apply=%region_2.3 | all-reduce | flops 1024 | bytes 8192 | tf_op jit(solution)/shard_map/psum | solution.py:80
  162.7 0.6 multiply_add_fusion
  163.4 12.3 %reduce-scatter.2.cloned.1.call-done = f32[1024,384]{1,0:T(8,128)} async-done(((f32[1024,768]{1,0:T(8,128)}), f32[1024,384]{1,0:T(8,128)}) %reduce-scatter.2.cloned.1.call-update) | async-done | bytes 1572880 | tf_op jit(solution)/shard_map/reduce_scatter | solution.py:79
  175.7 2.5 %divide_convert_fusion = bf16[1024,384]{1,0:T(8,128)(2,1)} fusion(f32[1024,384]{1,0:T(8,128)} %reduce-scatter.2.cloned.1.call-done, f32[1024]{0:T(1024)S(1)} %psum.7), kind=kLoop, calls=%fused_computation.10 | loop fusion | flops 786432 | bytes 2363392 | tf_op jit(solution)/shard_map/convert_element_type | solution.py:81
  (41 shorter events, 3.1 us)
Async XLA Ops:
  7.2 38.8 %all-gather.2.cloned.1.call-start = ((), (), s32[]{:S(2)}) async-start(), calls=%async_computation.1 | async-start | bytes 2359296 | tf_op jit(solution)/shard_map/all_gather | solution.py:47
  7.9 167.8 %reduce-scatter.2.cloned.1.call-start = ((), (), s32[]{:S(2)}) async-start(), calls=%async_computation.2 | async-start | bytes 4718592 | tf_op jit(solution)/shard_map/reduce_scatter | solution.py:79
  45.9 1.9 %copy-start.6 = (bf16[1024,768]{1,0:T(8,128)(2,1)S(1)}, bf16[1024,768]{1,0:T(8,128)(2,1)}, u32[]{:S(2)}) copy-start(bf16[1024,768]{1,0:T(8,128)(2,1)} %all-gather.2.cloned.1.call-done) | copy-start | bytes 4718596
  48.5 11.6 %collective-permute-start = (bf16[512,768]{1,0:T(8,128)(2,1)S(1)}, bf16[512,768]{1,0:T(8,128)(2,1)S(1)}, u32[]{:S(2)}, u32[]{:S(2)}) collective-permute-start(bf16[512,768]{1,0:T(8,128)(2,1)S(1)} %constant_dynamic-slice_fusion.1), channel_id=1, source_target_pairs={{0,254},{2,0},{4,2},{6,4},{8,6},{10,8},{12,10},{14,12},{16,14},{18... | collective-permute-start | bytes 2359304 | tf_op jit(solution)/shard_map/ppermute | solution.py:13
  49.3 19.2 %collective-permute-start.1 = (bf16[512,768]{1,0:T(8,128)(2,1)S(1)}, bf16[512,768]{1,0:T(8,128)(2,1)S(1)}, u32[]{:S(2)}, u32[]{:S(2)}) collective-permute-start(bf16[512,768]{1,0:T(8,128)(2,1)S(1)} %constant_dynamic-slice_fusion), channel_id=1, source_target_pairs={{0,254},{2,0},{4,2},{6,4},{8,6},{10,8},{12,10},{14,12},{16,14},{18... | collective-permute-start | bytes 2359304 | tf_op jit(solution)/shard_map/ppermute | solution.py:13
  60.1 16.9 %collective-permute-start.2 = (bf16[512,768]{1,0:T(8,128)(2,1)S(1)}, bf16[512,768]{1,0:T(8,128)(2,1)S(1)}, u32[]{:S(2)}, u32[]{:S(2)}) collective-permute-start(bf16[512,768]{1,0:T(8,128)(2,1)S(1)} %collective-permute-done), channel_id=1, source_target_pairs={{0,254},{2,0},{4,2},{6,4},{8,6},{10,8},{12,10},{14,12},{16,14},{18... | collective-permute-start | bytes 2359304 | tf_op jit(solution)/shard_map/ppermute | solution.py:13
  66.9 16.3 %copy-start.1 = (bf16[1024,512]{1,0:T(8,128)(2,1)}, bf16[1024,512]{1,0:T(8,128)(2,1)S(1)}, u32[]{:S(2)}) copy-start(bf16[1024,512]{1,0:T(8,128)(2,1)S(1)} %exponential_convert_fusion.1) | copy-start | bytes 3145732
  68.0 18.6 %collective-permute-start.4 = (f32[512,768]{1,0:T(8,128)S(1)}, f32[512,768]{1,0:T(8,128)S(1)}, u32[]{:S(2)}, u32[]{:S(2)}) collective-permute-start(f32[512,768]{1,0:T(8,128)S(1)} %fusion.4), channel_id=1, source_target_pairs={{0,2},{2,4},{4,6},{6,8},{8,10},{10,12},{12,14},{14,16},{16,18},{18... | collective-permute-start | bytes 4718600 | tf_op jit(solution)/shard_map/ppermute | solution.py:13
  68.5 17.1 %collective-permute-start.3 = (bf16[512,768]{1,0:T(8,128)(2,1)S(1)}, bf16[512,768]{1,0:T(8,128)(2,1)S(1)}, u32[]{:S(2)}, u32[]{:S(2)}) collective-permute-start(bf16[512,768]{1,0:T(8,128)(2,1)S(1)} %collective-permute-done.1), channel_id=1, source_target_pairs={{0,254},{2,0},{4,2},{6,4},{8,6},{10,8},{12,10},{14,12},{16,14},{18... | collective-permute-start | bytes 2359304 | tf_op jit(solution)/shard_map/ppermute | solution.py:13
  78.1 7.6 %copy-start.3 = (bf16[1024,512]{1,0:T(8,128)(2,1)}, bf16[1024,512]{1,0:T(8,128)(2,1)S(1)}, u32[]{:S(2)}) copy-start(bf16[1024,512]{1,0:T(8,128)(2,1)S(1)} %exponential_convert_fusion) | copy-start | bytes 3145732
  79.1 55.2 %collective-permute-start.5 = (f32[512,768]{1,0:T(8,128)S(1)}, f32[512,768]{1,0:T(8,128)S(1)}, u32[]{:S(2)}, u32[]{:S(2)}) collective-permute-start(f32[512,768]{1,0:T(8,128)S(1)} %fusion.5), channel_id=1, source_target_pairs={{0,4},{2,6},{4,8},{6,10},{8,12},{10,14},{12,16},{14,18},{16,20},{1... | collective-permute-start | bytes 4718600 | tf_op jit(solution)/shard_map/ppermute | solution.py:13
  82.2 2.0 %copy-start.5 = (bf16[1024,512]{1,0:T(8,128)(2,1)}, bf16[1024,512]{1,0:T(8,128)(2,1)S(1)}, u32[]{:S(2)}) copy-start(bf16[1024,512]{1,0:T(8,128)(2,1)S(1)} %select_convert_fusion) | copy-start | bytes 3145732
  134.7 1.7 copy-start
  134.7 1.7 copy-start.7
  136.4 9.6 %copy-start.2 = (bf16[1024,512]{1,0:T(8,128)(2,1)S(1)}, bf16[1024,512]{1,0:T(8,128)(2,1)}, u32[]{:S(2)}) copy-start(bf16[1024,512]{1,0:T(8,128)(2,1)} %copy-done.1) | copy-start | bytes 3145732
  136.4 10.0 %copy-start.4 = (bf16[1024,512]{1,0:T(8,128)(2,1)S(1)}, bf16[1024,512]{1,0:T(8,128)(2,1)}, u32[]{:S(2)}) copy-start(bf16[1024,512]{1,0:T(8,128)(2,1)} %copy-done.3) | copy-start | bytes 3145732
  136.5 3.0 %collective-permute-start.6 = (bf16[512]{0:T(512)(128)(2,1)S(1)}, bf16[512]{0:T(512)(128)(2,1)S(1)}, u32[]{:S(2)}, u32[]{:S(2)}) collective-permute-start(bf16[512]{0:T(512)(128)(2,1)S(1)} %dynamic_slice.18), channel_id=1, source_target_pairs={{0,254},{2,0},{4,2},{6,4},{8,6},{10,8},{12,10},{14,12},{16,14},{18... | collective-permute-start | bytes 3080 | tf_op jit(solution)/shard_map/ppermute | solution.py:13
  139.5 3.4 %collective-permute-start.7 = (bf16[512]{0:T(512)(128)(2,1)S(1)}, bf16[512]{0:T(512)(128)(2,1)S(1)}, u32[]{:S(2)}, u32[]{:S(2)}) collective-permute-start(bf16[512]{0:T(512)(128)(2,1)S(1)} %collective-permute-done.6), channel_id=1, source_target_pairs={{0,254},{2,0},{4,2},{6,4},{8,6},{10,8},{12,10},{14,12},{16,14},{18... | collective-permute-start | bytes 3080 | tf_op jit(solution)/shard_map/ppermute | solution.py:13
  146.0 4.2 %collective-permute-start.8 = (f32[512]{0:T(512)S(1)}, f32[512]{0:T(512)S(1)}, u32[]{:S(2)}, u32[]{:S(2)}) collective-permute-start(f32[512]{0:T(512)S(1)} %bitcast.34), channel_id=1, source_target_pairs={{0,2},{2,4},{4,6},{6,8},{8,10},{10,12},{12,14},{14,16},{16,18},{18... | collective-permute-start | bytes 6152 | tf_op jit(solution)/shard_map/ppermute | solution.py:13
  146.7 11.7 %collective-permute-start.9 = (f32[512]{0:T(512)S(1)}, f32[512]{0:T(512)S(1)}, u32[]{:S(2)}, u32[]{:S(2)}) collective-permute-start(f32[512]{0:T(512)S(1)} %bitcast.35), channel_id=1, source_target_pairs={{0,4},{2,6},{4,8},{6,10},{8,12},{10,14},{12,16},{14,18},{16,20},{1... | collective-permute-start | bytes 6152 | tf_op jit(solution)/shard_map/ppermute | solution.py:13
Sparse Core Ops, SparseCore 0:
  9.8 36.0 all-gather.1
  136.5 39.1 reduce-scatter.1
where the time goes:
time: 185 us
  waiting for transfers between devices  122 us (66%)
  starting transfers between devices  22.9 us (12%)
  between operations  14.3 us (8%)
  matrix products  12.7 us (7%)
  other arithmetic  6.86 us (4%)
  blocking collectives  4.22 us (2%)
  local copies, waits for them, and re-layouts  1.88 us (1%)
    ppermute x10, waiting for transfers between devices, passed_along(): return lax.ppermute(value, axis, pairs)  71.9 us
    all_gather x1, waiting for transfers between devices, shards(): gathered = lax.all_gather(embeddings, 'rep', axis=1, tiled=True)  37.3 us
    ppermute x10, starting transfers between devices, passed_along(): return lax.ppermute(value, axis, pairs)  22.8 us
    reduce_scatter x1, waiting for transfers between devices, shards(): lax.psum_scatter(row_sums, 'rep', scatter_dimension=1, tiled=True)  12.3 us
    psum x1, blocking collectives, shards(): total_mass = lax.psum(masses, 'rep')  4.22 us
  transfers between devices with their start and end apart: 12, of which 11 were waited for; matrix products, arithmetic and copies ran while one was open for 8% of the time, Pallas kernels for 0%

commit v1 on v0

v1 whole, which is shorter than its diff:
```python
import functools

import jax
import jax.numpy as jnp
from jax import lax
from jax.experimental import pallas as pl
from jax.experimental.pallas import tpu as pltpu
from jax.sharding import PartitionSpec as P

sharpness = 12.0
epsilon = 1e-06
LOG2E = 1.4426950408889634
QB = 256
WROWS = 16
RING = 16


def unit_scale(d0, d1):
    a = d0.astype(jnp.float32)
    b = d1.astype(jnp.float32)
    width = d0.shape[1] + d1.shape[1]
    total = jnp.sum(a * a, axis=1, keepdims=True) + jnp.sum(b * b, axis=1, keepdims=True)
    return a, b, lax.rsqrt(total / width + epsilon)


def log_weights(w_tile):
    logs = (jnp.log(w_tile.astype(jnp.float32)) - sharpness) * LOG2E
    return jnp.concatenate([logs[b : b + 1, :] for b in range(4)], axis=1)


def fill_keys(d0, d1, w_tile, flip, kn, bias):
    half = d0.shape[1]
    a, b, scale = unit_scale(d0, d1)
    first = pl.multiple_of(half - flip * half, half)
    second = pl.multiple_of(flip * half, half)
    kn[:, pl.ds(first, half)] = (a * scale).astype(jnp.bfloat16)
    kn[:, pl.ds(second, half)] = (b * scale).astype(jnp.bfloat16)
    kn[:, 2 * half :] = jnp.ones((kn.shape[0], kn.shape[1] - 2 * half), jnp.bfloat16)
    bias[...] = jnp.broadcast_to(log_weights(w_tile), bias.shape)


def add_slab(q, kn, bias, total, mask_from=None):
    half = kn.shape[1] // 7 * 3
    logits = lax.dot_general(
        q, kn[:, : 2 * half], (((1,), (1,)), ((), ())), preferred_element_type=jnp.float32
    )
    kernel = jnp.exp2(logits + bias[0:1, :])
    if mask_from is not None:
        rows = lax.broadcasted_iota(jnp.int32, kernel.shape, 0) + mask_from
        cols = lax.broadcasted_iota(jnp.int32, kernel.shape, 1)
        kernel = jnp.where(rows == cols, 0.0, kernel)
    return total + jnp.dot(
        kernel.astype(jnp.bfloat16), kn[:, half:], preferred_element_type=jnp.float32
    )


def first_kernel(e_ref, o_ref, se_ref, so_ref, q_ref, acc_ref, kn0, kn1, bias0, bias1, q_all):
    i = pl.program_id(0)
    half = e_ref.shape[1]

    @pl.when(i == 0)
    def _():
        fill_keys(e_ref[...], o_ref[WROWS:, :], o_ref[0:WROWS, 0:256], 0, kn0, bias0)
        fill_keys(se_ref[...], so_ref[WROWS:, :], so_ref[0:WROWS, 0:256], 0, kn1, bias1)
        factor = sharpness * LOG2E / (2 * half)
        q_all[...] = (kn0[:, : 2 * half].astype(jnp.float32) * factor).astype(jnp.bfloat16)

    q = q_all[pl.ds(pl.multiple_of(i * QB, QB), QB), :]
    q_ref[...] = q
    total = jnp.zeros(acc_ref.shape, jnp.float32)
    total = add_slab(q, kn0, bias0, total, i * QB)
    acc_ref[...] = add_slab(q, kn1, bias1, total)


def middle_kernel(flips, q_ref, acc_in, i0_ref, i1_ref, s0_ref, s1_ref, acc_ref, kn0, kn1, bias0, bias1):
    @pl.when(pl.program_id(0) == 0)
    def _():
        fill_keys(i0_ref[...], i1_ref[WROWS:, :], i1_ref[0:WROWS, 0:256], flips[0], kn0, bias0)
        fill_keys(s0_ref[...], s1_ref[WROWS:, :], s1_ref[0:WROWS, 0:256], flips[1], kn1, bias1)

    total = add_slab(q_ref[...], kn0, bias0, acc_in[...])
    acc_ref[...] = add_slab(q_ref[...], kn1, bias1, total)


def last_kernel(flips, q_ref, acc_in, d0_ref, front_ref, back_ref, out_ref, score_ref, kn0, bias0):
    i = pl.program_id(0)
    half = d0_ref.shape[1]

    @pl.when(i == 0)
    def _():
        d1 = jnp.concatenate([back_ref[...], front_ref[WROWS:, :]], axis=0)
        fill_keys(d0_ref[...], d1, front_ref[0:WROWS, 0:256], flips[1], kn0, bias0)

    total = add_slab(q_ref[...], kn0, bias0, acc_in[...])
    mass = total[:, half:]
    out_ref[...] = (total[:, :half] / jnp.concatenate([mass] * 3, axis=1)).astype(jnp.bfloat16)
    logs = jnp.log(mass) / sharpness + 1.0
    eye = lax.broadcasted_iota(jnp.int32, (128, 128), 0) == lax.broadcasted_iota(jnp.int32, (128, 128), 1)
    lines = [
        jnp.sum(jnp.where(eye, logs[b * 128 : (b + 1) * 128, :], 0.0), axis=0, keepdims=True)
        for b in range(QB // 128)
    ]
    score_ref[...] = jnp.concatenate(lines, axis=0).reshape(score_ref.shape)


def shards(embeddings, weights):
    rows, half = embeddings.shape
    count = lax.axis_size("blk")
    slab = lax.axis_index("blk")
    wide = half // 3 * 4

    def signed(step):
        pairs = []
        for to in range(count):
            source = (to + (step if to % 2 == 0 else -step)) % count
            flip = int(source // RING != to // RING)
            for r in range(2):
                pairs.append((source * 2 + r, to * 2 + (r ^ flip)))
        return pairs

    inner = signed(2)
    outer = signed(-2)
    over = lambda value, pairs: lax.ppermute(value, ("blk", "rep"), pairs)
    swap = lambda value: lax.ppermute(value, "blk", [(s, s ^ 1) for s in range(count)])
    trade = lambda value: lax.ppermute(value, "rep", [(0, 1), (1, 0)])

    sign = 1 - 2 * (slab % 2)
    wraps = lambda step: ((slab + step * sign) % count // RING != slab // RING).astype(jnp.int32)
    flips = jnp.stack([wraps(2), wraps(-2)])

    packed = jnp.full((WROWS, half), 1.0, jnp.bfloat16).at[:4, :256].set(weights.reshape(4, 256))
    other = trade(jnp.concatenate([packed, embeddings], axis=0))
    inner0 = over(embeddings, inner)
    outer0 = over(embeddings, outer)
    swapped0 = swap(embeddings)
    swapped1 = swap(other)
    inner1 = over(other, inner)
    cut = rows // 2
    outer1_front = over(jnp.concatenate([other[:WROWS], other[WROWS + cut :]], axis=0), outer)
    outer1_back = trade(outer0[:cut])
    mate0 = swap(inner0)
    mate1 = swap(inner1)

    steps = rows // QB
    whole = lambda shape: pl.BlockSpec(shape, lambda i, *_: (0,) * len(shape))
    block = lambda width: pl.BlockSpec((QB, width), lambda i, *_: (i, 0))
    keys = [pltpu.VMEM((rows, 7 * half // 3), jnp.bfloat16)]
    bias = [pltpu.VMEM((8, rows), jnp.float32)]
    params = pltpu.CompilerParams(vmem_limit_bytes=40 * 1024 * 1024, dimension_semantics=("arbitrary",))
    full0, full1 = whole((rows, half)), whole((rows + WROWS, half))

    queries, acc = pl.pallas_call(
        first_kernel,
        grid=(steps,),
        in_specs=[full0, full1, full0, full1],
        out_specs=[block(2 * half), block(wide)],
        out_shape=[
            jax.ShapeDtypeStruct((rows, 2 * half), jnp.bfloat16),
            jax.ShapeDtypeStruct((rows, wide), jnp.float32),
        ],
        scratch_shapes=keys * 2 + bias * 2 + [pltpu.VMEM((rows, 2 * half), jnp.bfloat16)],
        compiler_params=params,
        name="own_pair",
    )(embeddings, other, swapped0, swapped1)

    acc = pl.pallas_call(
        middle_kernel,
        grid_spec=pltpu.PrefetchScalarGridSpec(
            num_scalar_prefetch=1,
            grid=(steps,),
            in_specs=[block(2 * half), block(wide), full0, full1, full0, full1],
            out_specs=block(wide),
            scratch_shapes=keys * 2 + bias * 2,
        ),
        out_shape=jax.ShapeDtypeStruct((rows, wide), jnp.float32),
        compiler_params=params,
        name="inner_pair",
    )(flips, queries, acc, inner0, inner1, mate0, mate1)

    neighbours, scores = pl.pallas_call(
        last_kernel,
        grid_spec=pltpu.PrefetchScalarGridSpec(
            num_scalar_prefetch=1,
            grid=(steps,),
            in_specs=[
                block(2 * half),
                block(wide),
                full0,
                whole((rows - cut + WROWS, half)),
                whole((cut, half)),
            ],
            out_specs=[block(half), pl.BlockSpec((1, QB // 128, 128), lambda i, *_: (i, 0, 0))],
            scratch_shapes=keys + bias,
        ),
        out_shape=[
            jax.ShapeDtypeStruct((rows, half), jnp.bfloat16),
            jax.ShapeDtypeStruct((steps, QB // 128, 128), jnp.float32),
        ],
        compiler_params=params,
        name="outer_slab",
    )(flips, queries, acc, outer0, outer1_front, outer1_back)
    return neighbours, scores.reshape(rows)


def solution(mesh):
    return jax.shard_map(
        shards,
        mesh=mesh,
        in_specs=(P("blk", "rep"), P("blk")),
        out_specs=(P("blk", "rep"), P("blk")),
        check_vma=False,
    )
```

time: 185 us -> 95 us (0.51)
  waiting for transfers between devices: 122 us -> 28.7 us
  Pallas kernels: 0 us -> 24.4 us
  between operations: 14.3 us -> 0.71 us
  matrix products: 12.7 us -> 0 us
  starting transfers between devices: 22.9 us -> 35.4 us
  other arithmetic: 6.86 us -> 2.09 us
  blocking collectives: 4.22 us -> 0 us
    ppermute x10, waiting for transfers between devices: 71.9 us -> 28.7 us  [the longest x2 16.3 us: shards(): trade = lambda value: lax.ppermute(value, 'rep', [(0, 1), (1, 0)])]
    all_gather x1 -> x0, waiting for transfers between devices: 37.3 us -> none  [shards(): gathered = lax.all_gather(embeddings, 'rep', axis=1, tiled=True)]
    pallas_call x0 -> x3, Pallas kernels: none -> 24.4 us  [the longest x1 9.96 us: shards(): pl.pallas_call(middle_kernel, grid_spec=pltpu.PrefetchScalarGridSpec(num_...]
    dot_general x13 -> x0, matrix products: 12.7 us -> none  [the longest x3 3.57 us: kernel_of(): lax.dot_general(queries, keys_unit, (((1,), (1,)), ((), ())), preferred_e...]
    ppermute x10, starting transfers between devices: 22.8 us -> 35.4 us  [the longest x4 19 us: shards(): over = lambda value, pairs: lax.ppermute(value, ('blk', 'rep'), pairs)]
    reduce_scatter x1 -> x0, waiting for transfers between devices: 12.3 us -> none  [shards(): lax.psum_scatter(row_sums, 'rep', scatter_dimension=1, tiled=True)]
    psum x1 -> x0, blocking collectives: 4.22 us -> none  [shards(): total_mass = lax.psum(masses, 'rep')]
    convert_element_type x3 -> x0, other arithmetic: 3.71 us -> none  [the longest x1 2.5 us: shards(): neighbours = (feature_sums / total_mass[:, None]).astype(jnp.bfloat16)]
  transfers between devices with their start and end apart: 12 -> 10, of which waited for: 11 -> 3; matrix products, arithmetic and copies ran while one was open for 8% -> 2% of each run, Pallas kernels for 0% -> 19%
where the time goes in v1:
time: 95 us; the launch traced here: 94.8 us
  starting transfers between devices  35.4 us (37%)
  waiting for transfers between devices  28.7 us (30%)
  Pallas kernels  24.4 us (26%)
  local copies, waits for them, and re-layouts  3.55 us (4%)
  other arithmetic  2.09 us (2%)
    ppermute x4, starting transfers between devices, shards(): over = lambda value, pairs: lax.ppermute(value, ('blk', 'rep'), pairs)  19 us
    ppermute x2, waiting for transfers between devices, shards(): trade = lambda value: lax.ppermute(value, 'rep', [(0, 1), (1, 0)])  16.3 us
    ppermute x4, starting transfers between devices, shards(): lax.ppermute(value, 'blk', [(s, s ^ 1) for s in range(count)])  14.2 us
    ppermute x4, waiting for transfers between devices, shards(): over = lambda value, pairs: lax.ppermute(value, ('blk', 'rep'), pairs)  12.4 us
    pallas_call x1, Pallas kernels, shards(): pl.pallas_call(middle_kernel, grid_spec=pltpu.PrefetchScalarGridSpec(num_...  9.96 us
    pallas_call x1, Pallas kernels, shards(): pl.pallas_call(first_kernel, grid=(steps,), in_specs=[full0, full1, full0...  7.77 us
    pallas_call x1, Pallas kernels, shards(): pl.pallas_call(last_kernel, grid_spec=pltpu.PrefetchScalarGridSpec(num_sc...  6.65 us
    ppermute x2, starting transfers between devices, shards(): trade = lambda value: lax.ppermute(value, 'rep', [(0, 1), (1, 0)])  2.22 us
  transfers between devices with their start and end apart: 10, of which 3 were waited for; matrix products, arithmetic and copies ran while one was open for 2% of the time, Pallas kernels for 19%

profile of v1, /device:TPU:1, one launch (start us, length us, event | category | flops | bytes accessed | tf_op | source)
XLA Modules:
  0.0 94.8 jit_solution(17779017491601884535)
XLA Ops:
  0.6 0.7 reshape.41
  1.3 1.2 %fusion.1 = bf16[1040,384]{1,0:T(8,128)(2,1)S(1)} fusion(bf16[4,256]{1,0:T(4,128)(2,1)S(1)} %reshape.41, bf16[1024,384]{1,0:T(8,128)(2,1)} %e_ref.1), kind=kLoop, calls=%fused_computation.2 | loop fusion | flops 2396160 | bytes 1587200 | tf_op jit(solution)/shard_map/concatenate | solution.py:132
  2.5 0.0 copy-start
  2.5 2.2 %collective-permute-start = (bf16[1040,384]{1,0:T(8,128)(2,1)S(1)}, bf16[1040,384]{1,0:T(8,128)(2,1)S(1)}, u32[]{:S(2)}, u32[]{:S(2)}) collective-permute-start(bf16[1040,384]{1,0:T(8,128)(2,1)S(1)} %fusion.1), channel_id=1, source_target_pairs={{0,1},{1,0},{2,3},{3,2},{4,5},{5,4},{6,7},{7,6},{8,9},{9,8},{10,11... | collective-permute-start | bytes 2396168 | tf_op jit(solution)/shard_map/ppermute | solution.py:125
  4.8 16.3 %collective-permute-done.o_ref = bf16[1040,384]{1,0:T(8,128)(2,1)S(1)} collective-permute-done((bf16[1040,384]{1,0:T(8,128)(2,1)S(1)}, bf16[1040,384]{1,0:T(8,128)(2,1)S(1)}, u32[]{:S(2)}, u32[]{:S(2)}) %collective-permute-start) | collective-permute-done | bytes 798752 | tf_op jit(solution)/shard_map/ppermute | solution.py:125
  21.0 2.7 %collective-permute-start.4 = (bf16[1040,384]{1,0:T(8,128)(2,1)S(1)}, bf16[1040,384]{1,0:T(8,128)(2,1)}, u32[]{:S(2)}, u32[]{:S(2)}) collective-permute-start(bf16[1040,384]{1,0:T(8,128)(2,1)S(1)} %collective-permute-done.o_ref), channel_id=1, source_target_pairs={{4,0},{5,1},{254,3},{255,2},{8,4},{9,5},{2,6},{3,7},{12,8},{13,9},... | collective-permute-start | bytes 2396168 | tf_op jit(solution)/shard_map/ppermute | solution.py:123
  23.8 1.6 %collective-permute-start.3 = (bf16[1024,384]{1,0:T(8,128)(2,1)}, bf16[1024,384]{1,0:T(8,128)(2,1)}, u32[]{:S(2)}, u32[]{:S(2)}) collective-permute-start(bf16[1024,384]{1,0:T(8,128)(2,1)} %e_ref.1), channel_id=1, source_target_pairs={{4,0},{5,1},{254,3},{255,2},{8,4},{9,5},{2,6},{3,7},{12,8},{13,9},... | collective-permute-start | bytes 2359304 | tf_op jit(solution)/shard_map/ppermute | solution.py:123
  25.4 7.0 %collective-permute-start.7 = (bf16[1024,384]{1,0:T(8,128)(2,1)}, bf16[1024,384]{1,0:T(8,128)(2,1)S(1)}, u32[]{:S(2)}, u32[]{:S(2)}) collective-permute-start(bf16[1024,384]{1,0:T(8,128)(2,1)} %e_ref.1), channel_id=1, source_target_pairs={{252,1},{253,0},{6,2},{7,3},{0,4},{1,5},{10,6},{11,7},{4,8},{5,9},... | collective-permute-start | bytes 2359304 | tf_op jit(solution)/shard_map/ppermute | solution.py:123
  32.4 3.8 %collective-permute-start.1 = (bf16[1024,384]{1,0:T(8,128)(2,1)}, bf16[1024,384]{1,0:T(8,128)(2,1)S(1)}, u32[]{:S(2)}, u32[]{:S(2)}) collective-permute-start(bf16[1024,384]{1,0:T(8,128)(2,1)} %e_ref.1), channel_id=1, source_target_pairs={{0,2},{2,0},{4,6},{6,4},{8,10},{10,8},{12,14},{14,12},{16,18},{18,... | collective-permute-start | bytes 2359304 | tf_op jit(solution)/shard_map/ppermute | solution.py:124
  36.2 0.0 collective-permute-start.2
  36.2 5.8 %collective-permute-done.4.i1_ref = bf16[1040,384]{1,0:T(8,128)(2,1)} collective-permute-done((bf16[1040,384]{1,0:T(8,128)(2,1)S(1)}, bf16[1040,384]{1,0:T(8,128)(2,1)}, u32[]{:S(2)}, u32[]{:S(2)}) %collective-permute-start.4) | collective-permute-done | bytes 798752 | tf_op jit(solution)/shard_map/ppermute | solution.py:123
  42.0 8.5 %collective-permute-start.6 = (bf16[1040,384]{1,0:T(8,128)(2,1)}, bf16[1040,384]{1,0:T(8,128)(2,1)}, u32[]{:S(2)}, u32[]{:S(2)}) collective-permute-start(bf16[1040,384]{1,0:T(8,128)(2,1)} %collective-permute-done.4.i1_ref), channel_id=1, source_target_pairs={{0,2},{2,0},{4,6},{6,4},{8,10},{10,8},{12,14},{14,12},{16,18},{18,... | collective-permute-start | bytes 2396168 | tf_op jit(solution)/shard_map/ppermute | solution.py:124
  50.5 6.6 %collective-permute-done.3.i0_ref = bf16[1024,384]{1,0:T(8,128)(2,1)} collective-permute-done((bf16[1024,384]{1,0:T(8,128)(2,1)}, bf16[1024,384]{1,0:T(8,128)(2,1)}, u32[]{:S(2)}, u32[]{:S(2)}) %collective-permute-start.3) | collective-permute-done | bytes 786464 | tf_op jit(solution)/shard_map/ppermute | solution.py:123
  57.1 1.9 %collective-permute-start.5 = (bf16[1024,384]{1,0:T(8,128)(2,1)}, bf16[1024,384]{1,0:T(8,128)(2,1)}, u32[]{:S(2)}, u32[]{:S(2)}) collective-permute-start(bf16[1024,384]{1,0:T(8,128)(2,1)} %collective-permute-done.3.i0_ref), channel_id=1, source_target_pairs={{0,2},{2,0},{4,6},{6,4},{8,10},{10,8},{12,14},{14,12},{16,18},{18,... | collective-permute-start | bytes 2359304 | tf_op jit(solution)/shard_map/ppermute | solution.py:124
  59.1 0.8 pad_maximum_fusion
  59.9 0.0 collective-permute-done.7.d0_ref
  59.9 7.6 %collective-permute-start.8 = (bf16[528,384]{1,0:T(8,128)(2,1)}, bf16[528,384]{1,0:T(8,128)(2,1)}, u32[]{:S(2)}, u32[]{:S(2)}) collective-permute-start(bf16[528,384]{1,0:T(8,128)(2,1)} %pad_maximum_fusion), channel_id=1, source_target_pairs={{252,1},{253,0},{6,2},{7,3},{0,4},{1,5},{10,6},{11,7},{4,8},{5,9},... | collective-permute-start | bytes 1216520 | tf_op jit(solution)/shard_map/ppermute | solution.py:123
  67.5 0.8 slice.34
  68.3 0.0 collective-permute-done.1.se_ref
  68.3 0.9 copy-done.1
  69.2 0.0 collective-permute-start.9
  69.2 0.1 add_convert_fusion.flips
  69.2 0.0 collective-permute-done.2.so_ref
  69.2 0.0 copy-done
  69.3 1.1 %copy-done.2 = bf16[1024,384]{1,0:T(8,128)(2,1)S(1)} copy-done((bf16[1024,384]{1,0:T(8,128)(2,1)S(1)}, bf16[1024,384]{1,0:T(8,128)(2,1)}, u32[]{:S(2)}) %copy-start.2) | copy-done | bytes 786456
  70.4 7.8 %own_pair.1 = (bf16[1024,768]{1,0:T(8,128)(2,1)S(1)}, f32[1024,512]{1,0:T(8,128)S(1)}) custom-call(bf16[1024,384]{1,0:T(8,128)(2,1)S(1)} %copy-done, bf16[1040,384]{1,0:T(8,128)(2,1)S(1)} %collective-permute-done.o_ref, bf16[1024,384]{1,0:T(8,128)(2,1)S(1)} %copy-done.2, bf16[1040,384]{1,0:T(8,128)(2,1)S(1)} %collective-permute-done.2.so_ref), custom_call_target="tpu_custom_call" | custom-call | tf_op jit(solution)/shard_map/own_pair/pallas_call | solution.py:152
  78.2 0.0 collective-permute-done.5.s0_ref
  78.2 0.0 collective-permute-done.6.s1_ref
  78.2 10.0 %inner_pair.1.acc_in = f32[1024,512]{1,0:T(8,128)S(1)} custom-call(s32[2]{0:T(128)S(1)} %add_convert_fusion.flips, bf16[1024,768]{1,0:T(8,128)(2,1)S(1)} %get-tuple-element.18.q_ref, f32[1024,512]{1,0:T(8,128)S(1)} %get-tuple-element.19.acc_in, bf16[1024,384]{1,0:T(8,128)(2,1)} %collective-permute-done.3.i0_ref, ...), custom_call_target="tpu_custom_call" | custom-call | tf_op jit(solution)/shard_map/inner_pair/pallas_call | solution.py:166
  88.1 0.0 collective-permute-done.9.back_ref
  88.2 0.0 collective-permute-done.8.front_ref
  88.2 6.6 %outer_slab.1 = (bf16[1024,384]{1,0:T(8,128)(2,1)}, f32[4,2,128]{2,1,0:T(2,128)}) custom-call(s32[2]{0:T(128)S(1)} %add_convert_fusion.flips, bf16[1024,768]{1,0:T(8,128)(2,1)S(1)} %get-tuple-element.18.q_ref, f32[1024,512]{1,0:T(8,128)S(1)} %inner_pair.1.acc_in, bf16[1024,384]{1,0:T(8,128)(2,1)S(1)} %collective-permute-done.7.d0_ref, ...), custom_call_target="tpu_custom_call" | custom-call | tf_op jit(solution)/shard_map/outer_slab/pallas_call | solution.py:180
  (4 shorter events, 0.0 us)
Async XLA Ops:
  2.5 66.7 %copy-start = (bf16[1024,384]{1,0:T(8,128)(2,1)S(1)}, bf16[1024,384]{1,0:T(8,128)(2,1)}, u32[]{:S(2)}) copy-start(bf16[1024,384]{1,0:T(8,128)(2,1)} %e_ref.1) | copy-start | bytes 2359300
  2.5 18.5 %collective-permute-start = (bf16[1040,384]{1,0:T(8,128)(2,1)S(1)}, bf16[1040,384]{1,0:T(8,128)(2,1)S(1)}, u32[]{:S(2)}, u32[]{:S(2)}) collective-permute-start(bf16[1040,384]{1,0:T(8,128)(2,1)S(1)} %fusion.1), channel_id=1, source_target_pairs={{0,1},{1,0},{2,3},{3,2},{4,5},{5,4},{6,7},{7,6},{8,9},{9,8},{10,11... | collective-permute-start | bytes 2396168 | tf_op jit(solution)/shard_map/ppermute | solution.py:125
  21.0 20.9 %collective-permute-start.4 = (bf16[1040,384]{1,0:T(8,128)(2,1)S(1)}, bf16[1040,384]{1,0:T(8,128)(2,1)}, u32[]{:S(2)}, u32[]{:S(2)}) collective-permute-start(bf16[1040,384]{1,0:T(8,128)(2,1)S(1)} %collective-permute-done.o_ref), channel_id=1, source_target_pairs={{4,0},{5,1},{254,3},{255,2},{8,4},{9,5},{2,6},{3,7},{12,8},{13,9},... | collective-permute-start | bytes 2396168 | tf_op jit(solution)/shard_map/ppermute | solution.py:123
  23.8 33.3 %collective-permute-start.3 = (bf16[1024,384]{1,0:T(8,128)(2,1)}, bf16[1024,384]{1,0:T(8,128)(2,1)}, u32[]{:S(2)}, u32[]{:S(2)}) collective-permute-start(bf16[1024,384]{1,0:T(8,128)(2,1)} %e_ref.1), channel_id=1, source_target_pairs={{4,0},{5,1},{254,3},{255,2},{8,4},{9,5},{2,6},{3,7},{12,8},{13,9},... | collective-permute-start | bytes 2359304 | tf_op jit(solution)/shard_map/ppermute | solution.py:123
  25.4 34.4 %collective-permute-start.7 = (bf16[1024,384]{1,0:T(8,128)(2,1)}, bf16[1024,384]{1,0:T(8,128)(2,1)S(1)}, u32[]{:S(2)}, u32[]{:S(2)}) collective-permute-start(bf16[1024,384]{1,0:T(8,128)(2,1)} %e_ref.1), channel_id=1, source_target_pairs={{252,1},{253,0},{6,2},{7,3},{0,4},{1,5},{10,6},{11,7},{4,8},{5,9},... | collective-permute-start | bytes 2359304 | tf_op jit(solution)/shard_map/ppermute | solution.py:123
  32.4 35.9 %collective-permute-start.1 = (bf16[1024,384]{1,0:T(8,128)(2,1)}, bf16[1024,384]{1,0:T(8,128)(2,1)S(1)}, u32[]{:S(2)}, u32[]{:S(2)}) collective-permute-start(bf16[1024,384]{1,0:T(8,128)(2,1)} %e_ref.1), channel_id=1, source_target_pairs={{0,2},{2,0},{4,6},{6,4},{8,10},{10,8},{12,14},{14,12},{16,18},{18,... | collective-permute-start | bytes 2359304 | tf_op jit(solution)/shard_map/ppermute | solution.py:124
  36.2 33.0 %collective-permute-start.2 = (bf16[1040,384]{1,0:T(8,128)(2,1)S(1)}, bf16[1040,384]{1,0:T(8,128)(2,1)S(1)}, u32[]{:S(2)}, u32[]{:S(2)}) collective-permute-start(bf16[1040,384]{1,0:T(8,128)(2,1)S(1)} %collective-permute-done.o_ref), channel_id=1, source_target_pairs={{0,2},{2,0},{4,6},{6,4},{8,10},{10,8},{12,14},{14,12},{16,18},{18,... | collective-permute-start | bytes 2396168 | tf_op jit(solution)/shard_map/ppermute | solution.py:124
  42.0 36.2 %collective-permute-start.6 = (bf16[1040,384]{1,0:T(8,128)(2,1)}, bf16[1040,384]{1,0:T(8,128)(2,1)}, u32[]{:S(2)}, u32[]{:S(2)}) collective-permute-start(bf16[1040,384]{1,0:T(8,128)(2,1)} %collective-permute-done.4.i1_ref), channel_id=1, source_target_pairs={{0,2},{2,0},{4,6},{6,4},{8,10},{10,8},{12,14},{14,12},{16,18},{18,... | collective-permute-start | bytes 2396168 | tf_op jit(solution)/shard_map/ppermute | solution.py:124
  57.1 21.1 %collective-permute-start.5 = (bf16[1024,384]{1,0:T(8,128)(2,1)}, bf16[1024,384]{1,0:T(8,128)(2,1)}, u32[]{:S(2)}, u32[]{:S(2)}) collective-permute-start(bf16[1024,384]{1,0:T(8,128)(2,1)} %collective-permute-done.3.i0_ref), channel_id=1, source_target_pairs={{0,2},{2,0},{4,6},{6,4},{8,10},{10,8},{12,14},{14,12},{16,18},{18,... | collective-permute-start | bytes 2359304 | tf_op jit(solution)/shard_map/ppermute | solution.py:124
  59.9 28.3 %collective-permute-start.8 = (bf16[528,384]{1,0:T(8,128)(2,1)}, bf16[528,384]{1,0:T(8,128)(2,1)}, u32[]{:S(2)}, u32[]{:S(2)}) collective-permute-start(bf16[528,384]{1,0:T(8,128)(2,1)} %pad_maximum_fusion), channel_id=1, source_target_pairs={{252,1},{253,0},{6,2},{7,3},{0,4},{1,5},{10,6},{11,7},{4,8},{5,9},... | collective-permute-start | bytes 1216520 | tf_op jit(solution)/shard_map/ppermute | solution.py:123
  68.3 0.9 copy-start.1
  69.2 19.0 %collective-permute-start.9 = (bf16[512,384]{1,0:T(8,128)(2,1)}, bf16[512,384]{1,0:T(8,128)(2,1)}, u32[]{:S(2)}, u32[]{:S(2)}) collective-permute-start(bf16[512,384]{1,0:T(8,128)(2,1)} %slice.34), channel_id=1, source_target_pairs={{0,1},{1,0},{2,3},{3,2},{4,5},{5,4},{6,7},{7,6},{8,9},{9,8},{10,11... | collective-permute-start | bytes 1179656 | tf_op jit(solution)/shard_map/ppermute | solution.py:125
  69.3 1.1 %copy-start.2 = (bf16[1024,384]{1,0:T(8,128)(2,1)S(1)}, bf16[1024,384]{1,0:T(8,128)(2,1)}, u32[]{:S(2)}) copy-start(bf16[1024,384]{1,0:T(8,128)(2,1)} %copy-done.1) | copy-start | bytes 2359300

commit v2 on v0

v2 whole, which is shorter than its diff:
```python
import functools

import jax
import jax.numpy as jnp
from jax import lax
from jax.experimental import pallas as pl
from jax.experimental.pallas import tpu as pltpu
from jax.sharding import PartitionSpec as P
sharpness = 12.0
epsilon = 1e-06
LOG2E = 1.4426950408889634
WROWS = 16
RING = 16

def slab_kernel(*refs, sources, flip_ids, first, last, rows, half, KB, QB):
    refs = list(refs)
    flips = refs.pop(0)
    if not first:
        q_in, acc_in = refs.pop(0), refs.pop(0)
    n = len(sources)
    n_in = 1 + max(max([s["d0"], s["w"]] + [p[0] for p in s["d1"]]) for s in sources)
    ins = [refs.pop(0) for _ in range(n_in)]
    if last:
        out_ref, score_ref = refs.pop(0), refs.pop(0)
    else:
        q_out = refs.pop(0) if first else None
        acc_out = refs.pop(0)
    raw0, raw1, wt, kn, vals, q, acc, sems, qsem, asem, osem = refs
    copies = []
    for k, s in enumerate(sources):
        cs = [pltpu.make_async_copy(ins[s["d0"]], raw0.at[k], sems.at[k, 0])]
        for j, (ri, src, dst, cnt) in enumerate(s["d1"]):
            cs.append(pltpu.make_async_copy(ins[ri].at[pl.ds(src, cnt)], raw1.at[k, pl.ds(dst, cnt)], sems.at[k, 1 + j]))
        cs.append(pltpu.make_async_copy(ins[s["w"]].at[pl.ds(0, WROWS)], wt.at[k], sems.at[k, 3]))
        copies.append(cs)
    for c in copies[0]: c.start()
    if not first:
        cq = pltpu.make_async_copy(q_in, q, qsem); cq.start()
        ca = pltpu.make_async_copy(acc_in, acc, asem); ca.start()
    for cs in copies[1:]:
        for c in cs: c.start()
    wide = acc.shape[1]
    blocks = [(k, b) for k in range(n) for b in range(rows // KB)]
    eye = lax.broadcasted_iota(jnp.int32, (128, 128), 0) == lax.broadcasted_iota(jnp.int32, (128, 128), 1)

    def fill(index):
        k, b = blocks[index]
        slot = index % 2
        fid = flip_ids[k]
        for t in range(KB // 128):
            lo, r0 = t * 128, b * KB + t * 128
            line = r0 // 128
            a = raw0[k, r0:r0 + 128, :].astype(jnp.float32)
            o = raw1[k, r0:r0 + 128, :].astype(jnp.float32)
            tot = jnp.sum(a * a + o * o, axis=1, keepdims=True)
            sc = lax.rsqrt(tot / (2 * half) + epsilon)
            w_row = wt[k, 0:8, :128].astype(jnp.float32)[line:line + 1, :]
            w_col = jnp.sum(jnp.where(eye, w_row, 0.0), axis=1, keepdims=True)
            a = a * sc
            o = o * sc
            if fid is not None:
                sw = flips[fid] == 1
                a, o = jnp.where(sw, o, a), jnp.where(sw, a, o)
            kn[slot, lo:lo + 128, half:2 * half] = a.astype(jnp.bfloat16)
            kn[slot, lo:lo + 128, 0:half] = o.astype(jnp.bfloat16)
            vals[slot, lo:lo + 128, 0:half] = (a * w_col).astype(jnp.bfloat16)
            vals[slot, lo:lo + 128, half:wide] = jnp.broadcast_to(w_col, (128, wide - half)).astype(jnp.bfloat16)
            if first and k == 0:
                q[r0:r0 + 128, half:2 * half] = a.astype(jnp.bfloat16)
                q[r0:r0 + 128, 0:half] = o.astype(jnp.bfloat16)

    for c in copies[0]: c.wait()
    fill(0)
    ahead = first and len(blocks) > 1 and blocks[1][0] == 0
    if first:
        if ahead: fill(1)
    else:
        cq.wait(); ca.wait()
    waited = {0}
    nq = rows // QB
    factor = sharpness * LOG2E / (2 * half)
    for index, (k, b) in enumerate(blocks):
        if index + 1 < len(blocks) and not (ahead and index == 0):
            k2 = blocks[index + 1][0]
            if k2 not in waited:
                for c in copies[k2]: c.wait()
                waited.add(k2)
            fill(index + 1)
        slot = index % 2
        for i in range(nq):
            qs = slice(i * QB, (i + 1) * QB)
            logits = lax.dot_general(q[qs, :], kn[slot], (((1,), (1,)), ((), ())), preferred_element_type=jnp.float32)
            p = jnp.exp2(logits * factor - sharpness * LOG2E)
            if first and k == 0 and not ((i + 1) * QB <= b * KB or i * QB >= (b + 1) * KB):
                rr = lax.broadcasted_iota(jnp.int32, p.shape, 0) + i * QB
                cc = lax.broadcasted_iota(jnp.int32, p.shape, 1) + b * KB
                p = jnp.where(rr == cc, 0.0, p)
            pv = jnp.dot(p.astype(jnp.bfloat16), vals[slot], preferred_element_type=jnp.float32)
            if first and index == 0:
                acc[qs, :] = pv
            else:
                acc[qs, :] = acc[qs, :] + pv
            if index + 1 == len(blocks):
                if last:
                    for t in range(QB // 128):
                        ts = slice(i * QB + t * 128, i * QB + t * 128 + 128)
                        mass = acc[ts, half:]
                        inv = jnp.concatenate([mass] * (half // 128), axis=1)
                        out_ref[ts, :] = (acc[ts, :half] / inv).astype(jnp.bfloat16)
                        lg = jnp.log(mass) / sharpness + 1.0
                        score_ref[i * (QB // 128) + t, :] = jnp.sum(jnp.where(eye, lg, 0.0), axis=0)
                else:
                    pltpu.make_async_copy(acc.at[pl.ds(i * QB, QB)], acc_out.at[pl.ds(i * QB, QB)], osem.at[i]).start()
        if first and index == 0:
            cq = pltpu.make_async_copy(q, q_out, qsem); cq.start()
    if not last:
        for i in range(nq):
            pltpu.make_async_copy(acc.at[pl.ds(i * QB, QB)], acc_out.at[pl.ds(i * QB, QB)], osem.at[i]).wait()
    if first: cq.wait()

def slabs_call(flips, arrays, sources, flip_ids, rows, half, queries=None, acc=None, last=False, name="slabs", KB=1024, QB=512):
    first = queries is None
    n = len(sources)
    wide = half // 3 * 4
    anyspec = pl.BlockSpec(memory_space=pl.ANY)
    smem = pl.BlockSpec(memory_space=pltpu.SMEM)
    vm = pl.BlockSpec(memory_space=pltpu.VMEM)
    ops = [flips] + ([] if first else [queries, acc]) + list(arrays)
    specs = [smem] + [anyspec] * (len(ops) - 1)
    if last:
        outs = [jax.ShapeDtypeStruct((rows, half), jnp.bfloat16), jax.ShapeDtypeStruct((rows // 128, 128), jnp.float32)]
        ospecs = [vm, vm]
    else:
        outs = [jax.ShapeDtypeStruct((rows, wide), jnp.float32)]
        if first: outs = [jax.ShapeDtypeStruct((rows, 2 * half), jnp.bfloat16)] + outs
        ospecs = [anyspec] * len(outs)
    return pl.pallas_call(
        functools.partial(slab_kernel, sources=sources, first=first, last=last, rows=rows, half=half, flip_ids=flip_ids, KB=KB, QB=QB),
        in_specs=specs, out_specs=ospecs, out_shape=outs,
        scratch_shapes=[
            pltpu.VMEM((n, rows, half), jnp.bfloat16), pltpu.VMEM((n, rows, half), jnp.bfloat16),
            pltpu.VMEM((n, WROWS, half), jnp.bfloat16), pltpu.VMEM((2, KB, 2 * half), jnp.bfloat16),
            pltpu.VMEM((2, KB, wide), jnp.bfloat16),
            pltpu.VMEM((rows, 2 * half), jnp.bfloat16), pltpu.VMEM((rows, wide), jnp.float32),
            pltpu.SemaphoreType.DMA((n, 4)), pltpu.SemaphoreType.DMA, pltpu.SemaphoreType.DMA, pltpu.SemaphoreType.DMA((rows // QB,)),
        ],
        compiler_params=pltpu.CompilerParams(vmem_limit_bytes=48 * 1024 * 1024),
        name=name,
    )(*ops)


def shards(embeddings, weights):
    rows, half = embeddings.shape
    count = lax.axis_size("blk")
    slab = lax.axis_index("blk")

    def signed(step):
        pairs = []
        for to in range(count):
            source = (to + (step if to % 2 == 0 else -step)) % count
            flip = int(source // RING != to // RING)
            for r in range(2):
                pairs.append((source * 2 + r, to * 2 + (r ^ flip)))
        return pairs

    inner = signed(2)
    outer = signed(-2)
    over = lambda value, pairs: lax.ppermute(value, ("blk", "rep"), pairs)
    swap = lambda value: lax.ppermute(value, "blk", [(s, s ^ 1) for s in range(count)])
    trade = lambda value: lax.ppermute(value, "rep", [(0, 1), (1, 0)])

    sign = 1 - 2 * (slab % 2)
    wraps = lambda step: ((slab + step * sign) % count // RING != slab // RING).astype(jnp.int32)
    flips = jnp.stack([wraps(2), wraps(-2)])

    packed = jnp.full((WROWS, half), 1.0, jnp.bfloat16).at[:8, :128].set(weights.reshape(8, 128))
    inner0 = over(embeddings, inner)
    outer0 = over(embeddings, outer)
    swapped0 = swap(embeddings)
    other = trade(jnp.concatenate([packed, embeddings], axis=0))
    other, inner0, outer0, swapped0 = lax.optimization_barrier((other, inner0, outer0, swapped0))

    cut = rows // 2
    swapped1 = swap(other)
    inner1 = over(other, inner)
    mate0 = swap(inner0)
    outer1_back = trade(outer0[:cut])
    outer1_front = over(jnp.concatenate([other[:WROWS], other[WROWS + cut :]], axis=0), outer)

    whole = lambda first: {"d0": first, "d1": [(first + 1, WROWS, 0, rows)], "w": first + 1}
    queries, acc = slabs_call(
        flips, [embeddings, other, swapped0, swapped1], [whole(0), whole(2)], [None, None], rows, half, name="own_pair"
    )
    acc, inner1, outer1_back, outer1_front = lax.optimization_barrier((acc, inner1, outer1_back, outer1_front))
    mate1 = swap(inner1)
    (acc,) = slabs_call(
        flips, [inner0, inner1], [whole(0)], [0], rows, half, queries=queries, acc=acc, name="inner_slab"
    )
    halves = {"d0": 2, "d1": [(3, 0, 0, cut), (4, WROWS, cut, rows - cut)], "w": 4}
    neighbours, scores = slabs_call(
        flips,
        [mate0, mate1, outer0, outer1_back, outer1_front],
        [whole(0), halves],
        [1, 1],
        rows,
        half,
        queries=queries,
        acc=acc,
        last=True,
        name="last_pair",
    )
    return neighbours, scores.reshape(rows)


def solution(mesh):
    return jax.shard_map(
        shards,
        mesh=mesh,
        in_specs=(P("blk", "rep"), P("blk")),
        out_specs=(P("blk", "rep"), P("blk")),
        check_vma=False,
    )
```

time: 185 us -> 72.3 us (0.39)
  waiting for transfers between devices: 122 us -> 15.2 us
  Pallas kernels: 0 us -> 24.5 us
  between operations: 14.3 us -> 0.85 us
  matrix products: 12.7 us -> 0 us
  other arithmetic: 6.86 us -> 2.13 us
  blocking collectives: 4.22 us -> 0 us
  local copies, waits for them, and re-layouts: 1.88 us -> 4.2 us
  starting transfers between devices: 22.9 us -> 25.2 us
    ppermute x10, waiting for transfers between devices: 71.9 us -> 15.2 us  [the longest x4 15 us: shards(): over = lambda value, pairs: lax.ppermute(value, ('blk', 'rep'), pairs)]
    all_gather x1 -> x0, waiting for transfers between devices: 37.3 us -> none  [shards(): gathered = lax.all_gather(embeddings, 'rep', axis=1, tiled=True)]
    pallas_call x0 -> x3, Pallas kernels: none -> 24.5 us  [slabs_call(): pl.pallas_call(functools.partial(slab_kernel, sources=sources, first=firs...]
    dot_general x13 -> x0, matrix products: 12.7 us -> none  [the longest x3 3.57 us: kernel_of(): lax.dot_general(queries, keys_unit, (((1,), (1,)), ((), ())), preferred_e...]
    reduce_scatter x1 -> x0, waiting for transfers between devices: 12.3 us -> none  [shards(): lax.psum_scatter(row_sums, 'rep', scatter_dimension=1, tiled=True)]
    psum x1 -> x0, blocking collectives: 4.22 us -> none  [shards(): total_mass = lax.psum(masses, 'rep')]
    convert_element_type x3 -> x0, other arithmetic: 3.71 us -> none  [the longest x1 2.5 us: shards(): neighbours = (feature_sums / total_mass[:, None]).astype(jnp.bfloat16)]
    ppermute x10, starting transfers between devices: 22.8 us -> 25.2 us  [the longest x4 16.4 us: shards(): over = lambda value, pairs: lax.ppermute(value, ('blk', 'rep'), pairs)]
  transfers between devices with their start and end apart: 12 -> 10, of which waited for: 11 -> 3; matrix products, arithmetic and copies ran while one was open for 8% -> 2% of each run, Pallas kernels for 0% -> 21%
where the time goes in v2:
time: 72.3 us; the launch traced here: 72.1 us
  starting transfers between devices  25.2 us (35%)
  Pallas kernels  24.5 us (34%)
  waiting for transfers between devices  15.2 us (21%)
  local copies, waits for them, and re-layouts  4.2 us (6%)
  other arithmetic  2.13 us (3%)
  between operations  0.85 us (1%)
    pallas_call x3, Pallas kernels, slabs_call(): pl.pallas_call(functools.partial(slab_kernel, sources=sources, first=firs...  24.5 us
    ppermute x4, starting transfers between devices, shards(): over = lambda value, pairs: lax.ppermute(value, ('blk', 'rep'), pairs)  16.4 us
    ppermute x4, waiting for transfers between devices, shards(): over = lambda value, pairs: lax.ppermute(value, ('blk', 'rep'), pairs)  15 us
    ppermute x4, starting transfers between devices, shards(): lax.ppermute(value, 'blk', [(s, s ^ 1) for s in range(count)])  6.56 us
    unnamed x12, local copies, waits for them, and re-layouts  3.36 us
    ppermute x2, starting transfers between devices, shards(): trade = lambda value: lax.ppermute(value, 'rep', [(0, 1), (1, 0)])  2.22 us
  transfers between devices with their start and end apart: 10, of which 3 were waited for; matrix products, arithmetic and copies ran while one was open for 2% of the time, Pallas kernels for 21%

profile of v2, /device:TPU:1, one launch (start us, length us, event | category | flops | bytes accessed | tf_op | source)
XLA Modules:
  0.0 72.1 jit_solution(14131732256123491860)
XLA Ops:
  0.6 1.2 %fusion.1 = bf16[1040,384]{1,0:T(8,128)(2,1)S(1)} fusion(bf16[8,128]{1,0:T(8,128)(2,1)} %bitcast.4, bf16[1024,384]{1,0:T(8,128)(2,1)} %refs_1_.1), kind=kLoop, calls=%fused_computation.2 | loop fusion | flops 2396160 | bytes 1587200 | tf_op jit(solution)/shard_map/concatenate | solution.py:180
  1.9 0.0 copy-start.1
  1.9 2.2 %collective-permute-start = (bf16[1040,384]{1,0:T(8,128)(2,1)S(1)}, bf16[1040,384]{1,0:T(8,128)(2,1)S(1)}, u32[]{:S(2)}, u32[]{:S(2)}) collective-permute-start(bf16[1040,384]{1,0:T(8,128)(2,1)S(1)} %fusion.1), channel_id=1, source_target_pairs={{0,1},{1,0},{2,3},{3,2},{4,5},{5,4},{6,7},{7,6},{8,9},{9,8},{10,11... | collective-permute-start | bytes 2396168 | tf_op jit(solution)/shard_map/ppermute | solution.py:170
  4.1 1.6 %collective-permute-start.1 = (bf16[1024,384]{1,0:T(8,128)(2,1)}, bf16[1024,384]{1,0:T(8,128)(2,1)S(1)}, u32[]{:S(2)}, u32[]{:S(2)}) collective-permute-start(bf16[1024,384]{1,0:T(8,128)(2,1)} %refs_1_.1), channel_id=1, source_target_pairs={{4,0},{5,1},{254,3},{255,2},{8,4},{9,5},{2,6},{3,7},{12,8},{13,9},... | collective-permute-start | bytes 2359304 | tf_op jit(solution)/shard_map/ppermute | solution.py:168
  5.7 7.8 %collective-permute-start.2 = (bf16[1024,384]{1,0:T(8,128)(2,1)}, bf16[1024,384]{1,0:T(8,128)(2,1)S(1)}, u32[]{:S(2)}, u32[]{:S(2)}) collective-permute-start(bf16[1024,384]{1,0:T(8,128)(2,1)} %refs_1_.1), channel_id=1, source_target_pairs={{252,1},{253,0},{6,2},{7,3},{0,4},{1,5},{10,6},{11,7},{4,8},{5,9},... | collective-permute-start | bytes 2359304 | tf_op jit(solution)/shard_map/ppermute | solution.py:168
  13.5 1.2 %collective-permute-start.3 = (bf16[1024,384]{1,0:T(8,128)(2,1)}, bf16[1024,384]{1,0:T(8,128)(2,1)S(1)}, u32[]{:S(2)}, u32[]{:S(2)}) collective-permute-start(bf16[1024,384]{1,0:T(8,128)(2,1)} %refs_1_.1), channel_id=1, source_target_pairs={{0,2},{2,0},{4,6},{6,4},{8,10},{10,8},{12,14},{14,12},{16,18},{18,... | collective-permute-start | bytes 2359304 | tf_op jit(solution)/shard_map/ppermute | solution.py:169
  14.7 8.3 %collective-permute-done.1.refs_3_ = bf16[1024,384]{1,0:T(8,128)(2,1)S(1)} collective-permute-done((bf16[1024,384]{1,0:T(8,128)(2,1)}, bf16[1024,384]{1,0:T(8,128)(2,1)S(1)}, u32[]{:S(2)}, u32[]{:S(2)}) %collective-permute-start.1) | collective-permute-done | bytes 786464 | tf_op jit(solution)/shard_map/ppermute | solution.py:168
  23.1 6.6 %collective-permute-done.2.refs_5_ = bf16[1024,384]{1,0:T(8,128)(2,1)S(1)} collective-permute-done((bf16[1024,384]{1,0:T(8,128)(2,1)}, bf16[1024,384]{1,0:T(8,128)(2,1)S(1)}, u32[]{:S(2)}, u32[]{:S(2)}) %collective-permute-start.2) | collective-permute-done | bytes 786464 | tf_op jit(solution)/shard_map/ppermute | solution.py:168
  29.7 0.0 collective-permute-done.3.refs_3_
  29.7 0.9 %copy-done.2 = bf16[1024,384]{1,0:T(8,128)(2,1)} copy-done((bf16[1024,384]{1,0:T(8,128)(2,1)}, bf16[1024,384]{1,0:T(8,128)(2,1)S(1)}, u32[]{:S(2)}) %copy-start.2) | copy-done | bytes 786456
  30.6 0.0 collective-permute-done.refs_2_
  30.6 2.7 %collective-permute-start.4 = (bf16[1040,384]{1,0:T(8,128)(2,1)S(1)}, bf16[1040,384]{1,0:T(8,128)(2,1)}, u32[]{:S(2)}, u32[]{:S(2)}) collective-permute-start(bf16[1040,384]{1,0:T(8,128)(2,1)S(1)} %collective-permute-done.refs_2_), channel_id=1, source_target_pairs={{0,2},{2,0},{4,6},{6,4},{8,10},{10,8},{12,14},{14,12},{16,18},{18,... | collective-permute-start | bytes 2396168 | tf_op jit(solution)/shard_map/ppermute | solution.py:169
  33.2 0.0 collective-permute-start.5
  33.3 0.8 %pad_maximum_fusion = bf16[528,384]{1,0:T(8,128)(2,1)} fusion(bf16[512,384]{1,0:T(8,128)(2,1)S(1)} %slice.31, bf16[16,384]{1,0:T(8,128)(2,1)S(1)} %slice.30), kind=kLoop, calls=%fused_computation.3 | loop fusion | flops 811008 | bytes 811008 | tf_op jit(solution)/shard_map/concatenate | solution.py:188
  34.1 7.1 %collective-permute-start.7 = (bf16[528,384]{1,0:T(8,128)(2,1)}, bf16[528,384]{1,0:T(8,128)(2,1)}, u32[]{:S(2)}, u32[]{:S(2)}) collective-permute-start(bf16[528,384]{1,0:T(8,128)(2,1)} %pad_maximum_fusion), channel_id=1, source_target_pairs={{252,1},{253,0},{6,2},{7,3},{0,4},{1,5},{10,6},{11,7},{4,8},{5,9},... | collective-permute-start | bytes 1216520 | tf_op jit(solution)/shard_map/ppermute | solution.py:168
  41.2 0.8 %slice.29 = bf16[512,384]{1,0:T(8,128)(2,1)} slice(bf16[1024,384]{1,0:T(8,128)(2,1)S(1)} %collective-permute-done.2.refs_5_), slice={[0:512], [0:384]} | slice | bytes 786432 | tf_op jit(solution)/shard_map/slice | solution.py:187
  42.0 0.0 collective-permute-start.6
  42.0 0.1 add_convert_fusion.refs_0_
  42.0 0.0 collective-permute-done.4.refs_4_
  42.0 0.0 copy-done.1
  42.0 1.1 %copy-done.3 = bf16[1024,384]{1,0:T(8,128)(2,1)S(1)} copy-done((bf16[1024,384]{1,0:T(8,128)(2,1)S(1)}, bf16[1024,384]{1,0:T(8,128)(2,1)}, u32[]{:S(2)}) %copy-start.3) | copy-done | bytes 786456
  43.2 9.3 %own_pair.1 = (bf16[1024,768]{1,0:T(8,128)(2,1)S(1)}, f32[1024,512]{1,0:T(8,128)}) custom-call(s32[2]{0:T(128)S(1)} %add_convert_fusion.refs_0_, bf16[1024,384]{1,0:T(8,128)(2,1)S(1)} %copy-done.1, bf16[1040,384]{1,0:T(8,128)(2,1)S(1)} %collective-permute-done.refs_2_, bf16[1024,384]{1,0:T(8,128)(2,1)S(1)} %copy-done.3, ...), custom_call_target="tpu_custom_call" | custom-call | tf_op jit(solution)/shard_map/own_pair/pallas_call | solution.py:137
  52.5 0.2 collective-permute-done.6.refs_6_
  52.7 0.0 collective-permute-done.7.refs_7_
  52.7 0.0 collective-permute-done.5.refs_4_
  52.7 2.4 %collective-permute-start.9 = (bf16[1040,384]{1,0:T(8,128)(2,1)S(1)}, bf16[1040,384]{1,0:T(8,128)(2,1)S(1)}, u32[]{:S(2)}, u32[]{:S(2)}) collective-permute-start(bf16[1040,384]{1,0:T(8,128)(2,1)S(1)} %collective-permute-done.5.refs_4_), channel_id=1, source_target_pairs={{0,2},{2,0},{4,6},{6,4},{8,10},{10,8},{12,14},{14,12},{16,18},{18,... | collective-permute-start | bytes 2396168 | tf_op jit(solution)/shard_map/ppermute | solution.py:169
  55.1 0.3 collective-permute-start.8
  55.4 5.7 %inner_slab.1.refs_2_ = f32[1024,512]{1,0:T(8,128)S(1)} custom-call(s32[2]{0:T(128)S(1)} %add_convert_fusion.refs_0_, bf16[1024,768]{1,0:T(8,128)(2,1)S(1)} %get-tuple-element.28.refs_1_, f32[1024,512]{1,0:T(8,128)} %get-tuple-element.31.refs_2_, bf16[1024,384]{1,0:T(8,128)(2,1)S(1)} %copy-done.5, bf16[1040,384]{1,0:T(8,128)(2,1)S(1)} %collective-permute-done.5.refs_4_), custom_call_target="tpu_custom_call" | custom-call | tf_op jit(solution)/shard_map/inner_slab/pallas_call | solution.py:137
  61.1 1.3 %copy-done = f32[1024,512]{1,0:T(8,128)} copy-done((f32[1024,512]{1,0:T(8,128)}, f32[1024,512]{1,0:T(8,128)S(1)}, u32[]{:S(2)}) %copy-start) | copy-done | bytes 2097176
  62.5 0.0 collective-permute-done.8.refs_3_
  62.5 0.0 collective-permute-done.9.refs_4_
  62.5 9.5 %last_pair.1 = (bf16[1024,384]{1,0:T(8,128)(2,1)}, f32[8,128]{1,0:T(8,128)}) custom-call(s32[2]{0:T(128)S(1)} %add_convert_fusion.refs_0_, bf16[1024,768]{1,0:T(8,128)(2,1)S(1)} %get-tuple-element.28.refs_1_, f32[1024,512]{1,0:T(8,128)} %copy-done, bf16[1024,384]{1,0:T(8,128)(2,1)S(1)} %collective-permute-done.8.refs_3_, ...), custom_call_target="tpu_custom_call" | custom-call | tf_op jit(solution)/shard_map/last_pair/pallas_call | solution.py:137
  (9 shorter events, 0.1 us)
Async XLA Ops:
  1.9 40.2 %copy-start.1 = (bf16[1024,384]{1,0:T(8,128)(2,1)S(1)}, bf16[1024,384]{1,0:T(8,128)(2,1)}, u32[]{:S(2)}) copy-start(bf16[1024,384]{1,0:T(8,128)(2,1)} %refs_1_.1) | copy-start | bytes 2359300
  1.9 28.7 %collective-permute-start = (bf16[1040,384]{1,0:T(8,128)(2,1)S(1)}, bf16[1040,384]{1,0:T(8,128)(2,1)S(1)}, u32[]{:S(2)}, u32[]{:S(2)}) collective-permute-start(bf16[1040,384]{1,0:T(8,128)(2,1)S(1)} %fusion.1), channel_id=1, source_target_pairs={{0,1},{1,0},{2,3},{3,2},{4,5},{5,4},{6,7},{7,6},{8,9},{9,8},{10,11... | collective-permute-start | bytes 2396168 | tf_op jit(solution)/shard_map/ppermute | solution.py:170
  4.1 19.0 %collective-permute-start.1 = (bf16[1024,384]{1,0:T(8,128)(2,1)}, bf16[1024,384]{1,0:T(8,128)(2,1)S(1)}, u32[]{:S(2)}, u32[]{:S(2)}) collective-permute-start(bf16[1024,384]{1,0:T(8,128)(2,1)} %refs_1_.1), channel_id=1, source_target_pairs={{4,0},{5,1},{254,3},{255,2},{8,4},{9,5},{2,6},{3,7},{12,8},{13,9},... | collective-permute-start | bytes 2359304 | tf_op jit(solution)/shard_map/ppermute | solution.py:168
  5.7 24.0 %collective-permute-start.2 = (bf16[1024,384]{1,0:T(8,128)(2,1)}, bf16[1024,384]{1,0:T(8,128)(2,1)S(1)}, u32[]{:S(2)}, u32[]{:S(2)}) collective-permute-start(bf16[1024,384]{1,0:T(8,128)(2,1)} %refs_1_.1), channel_id=1, source_target_pairs={{252,1},{253,0},{6,2},{7,3},{0,4},{1,5},{10,6},{11,7},{4,8},{5,9},... | collective-permute-start | bytes 2359304 | tf_op jit(solution)/shard_map/ppermute | solution.py:168
  13.5 16.2 %collective-permute-start.3 = (bf16[1024,384]{1,0:T(8,128)(2,1)}, bf16[1024,384]{1,0:T(8,128)(2,1)S(1)}, u32[]{:S(2)}, u32[]{:S(2)}) collective-permute-start(bf16[1024,384]{1,0:T(8,128)(2,1)} %refs_1_.1), channel_id=1, source_target_pairs={{0,2},{2,0},{4,6},{6,4},{8,10},{10,8},{12,14},{14,12},{16,18},{18,... | collective-permute-start | bytes 2359304 | tf_op jit(solution)/shard_map/ppermute | solution.py:169
  23.1 7.5 %copy-start.4 = (bf16[1024,384]{1,0:T(8,128)(2,1)}, bf16[1024,384]{1,0:T(8,128)(2,1)S(1)}, u32[]{:S(2)}) copy-start(bf16[1024,384]{1,0:T(8,128)(2,1)S(1)} %collective-permute-done.1.refs_3_) | copy-start | bytes 2359300
  29.7 0.9 %copy-start.2 = (bf16[1024,384]{1,0:T(8,128)(2,1)}, bf16[1024,384]{1,0:T(8,128)(2,1)S(1)}, u32[]{:S(2)}) copy-start(bf16[1024,384]{1,0:T(8,128)(2,1)S(1)} %collective-permute-done.3.refs_3_) | copy-start | bytes 2359300
  30.6 11.5 %collective-permute-start.4 = (bf16[1040,384]{1,0:T(8,128)(2,1)S(1)}, bf16[1040,384]{1,0:T(8,128)(2,1)}, u32[]{:S(2)}, u32[]{:S(2)}) collective-permute-start(bf16[1040,384]{1,0:T(8,128)(2,1)S(1)} %collective-permute-done.refs_2_), channel_id=1, source_target_pairs={{0,2},{2,0},{4,6},{6,4},{8,10},{10,8},{12,14},{14,12},{16,18},{18,... | collective-permute-start | bytes 2396168 | tf_op jit(solution)/shard_map/ppermute | solution.py:169
  33.2 19.5 %collective-permute-start.5 = (bf16[1040,384]{1,0:T(8,128)(2,1)S(1)}, bf16[1040,384]{1,0:T(8,128)(2,1)S(1)}, u32[]{:S(2)}, u32[]{:S(2)}) collective-permute-start(bf16[1040,384]{1,0:T(8,128)(2,1)S(1)} %collective-permute-done.refs_2_), channel_id=1, source_target_pairs={{4,0},{5,1},{254,3},{255,2},{8,4},{9,5},{2,6},{3,7},{12,8},{13,9},... | collective-permute-start | bytes 2396168 | tf_op jit(solution)/shard_map/ppermute | solution.py:168
  34.1 18.6 %collective-permute-start.7 = (bf16[528,384]{1,0:T(8,128)(2,1)}, bf16[528,384]{1,0:T(8,128)(2,1)}, u32[]{:S(2)}, u32[]{:S(2)}) collective-permute-start(bf16[528,384]{1,0:T(8,128)(2,1)} %pad_maximum_fusion), channel_id=1, source_target_pairs={{252,1},{253,0},{6,2},{7,3},{0,4},{1,5},{10,6},{11,7},{4,8},{5,9},... | collective-permute-start | bytes 1216520 | tf_op jit(solution)/shard_map/ppermute | solution.py:168
  42.0 10.7 %collective-permute-start.6 = (bf16[512,384]{1,0:T(8,128)(2,1)}, bf16[512,384]{1,0:T(8,128)(2,1)}, u32[]{:S(2)}, u32[]{:S(2)}) collective-permute-start(bf16[512,384]{1,0:T(8,128)(2,1)} %slice.29), channel_id=1, source_target_pairs={{0,1},{1,0},{2,3},{3,2},{4,5},{5,4},{6,7},{7,6},{8,9},{9,8},{10,11... | collective-permute-start | bytes 1179656 | tf_op jit(solution)/shard_map/ppermute | solution.py:170
  42.0 1.1 %copy-start.3 = (bf16[1024,384]{1,0:T(8,128)(2,1)S(1)}, bf16[1024,384]{1,0:T(8,128)(2,1)}, u32[]{:S(2)}) copy-start(bf16[1024,384]{1,0:T(8,128)(2,1)} %copy-done.2) | copy-start | bytes 2359300
  43.2 11.9 %copy-start.5 = (bf16[1024,384]{1,0:T(8,128)(2,1)S(1)}, bf16[1024,384]{1,0:T(8,128)(2,1)}, u32[]{:S(2)}) copy-start(bf16[1024,384]{1,0:T(8,128)(2,1)} %copy-done.4) | copy-start | bytes 2359300
  52.7 9.8 %collective-permute-start.9 = (bf16[1040,384]{1,0:T(8,128)(2,1)S(1)}, bf16[1040,384]{1,0:T(8,128)(2,1)S(1)}, u32[]{:S(2)}, u32[]{:S(2)}) collective-permute-start(bf16[1040,384]{1,0:T(8,128)(2,1)S(1)} %collective-permute-done.5.refs_4_), channel_id=1, source_target_pairs={{0,2},{2,0},{4,6},{6,4},{8,10},{10,8},{12,14},{14,12},{16,18},{18,... | collective-permute-start | bytes 2396168 | tf_op jit(solution)/shard_map/ppermute | solution.py:169
  55.1 7.4 %collective-permute-start.8 = (bf16[1024,384]{1,0:T(8,128)(2,1)S(1)}, bf16[1024,384]{1,0:T(8,128)(2,1)S(1)}, u32[]{:S(2)}, u32[]{:S(2)}) collective-permute-start(bf16[1024,384]{1,0:T(8,128)(2,1)S(1)} %copy-done.5), channel_id=1, source_target_pairs={{0,2},{2,0},{4,6},{6,4},{8,10},{10,8},{12,14},{14,12},{16,18},{18,... | collective-permute-start | bytes 2359304 | tf_op jit(solution)/shard_map/ppermute | solution.py:169
  61.1 1.3 %copy-start = (f32[1024,512]{1,0:T(8,128)}, f32[1024,512]{1,0:T(8,128)S(1)}, u32[]{:S(2)}) copy-start(f32[1024,512]{1,0:T(8,128)S(1)} %inner_slab.1.refs_2_) | copy-start | bytes 6291460

commit v3 on v2

--- a/solution.py
+++ b/solution.py
@@ -25,7 +25,7 @@
     else:
         q_out = refs.pop(0) if first else None
         acc_out = refs.pop(0)
-    raw0, raw1, wt, kn, vals, q, acc, sems, qsem, asem, osem = refs
+    raw0, raw1, wt, kn, vals, q, acc, old, sems, qsem, asem, osem = refs
     copies = []
     for k, s in enumerate(sources):
         cs = [pltpu.make_async_copy(ins[s["d0"]], raw0.at[k], sems.at[k, 0])]
@@ -36,9 +36,11 @@
     for c in copies[0]: c.start()
     if not first:
         cq = pltpu.make_async_copy(q_in, q, qsem); cq.start()
-        ca = pltpu.make_async_copy(acc_in, acc, asem); ca.start()
+        ca = pltpu.make_async_copy(acc_in, old, asem)
     for cs in copies[1:]:
         for c in cs: c.start()
+    if not first:
+        ca.start()
     wide = acc.shape[1]
     blocks = [(k, b) for k in range(n) for b in range(rows // KB)]
     eye = lax.broadcasted_iota(jnp.int32, (128, 128), 0) == lax.broadcasted_iota(jnp.int32, (128, 128), 1)
@@ -75,7 +77,7 @@
     if first:
         if ahead: fill(1)
     else:
-        cq.wait(); ca.wait()
+        cq.wait()
     waited = {0}
     nq = rows // QB
     factor = sharpness * LOG2E / (2 * half)
@@ -96,10 +98,18 @@
                 cc = lax.broadcasted_iota(jnp.int32, p.shape, 1) + b * KB
                 p = jnp.where(rr == cc, 0.0, p)
             pv = jnp.dot(p.astype(jnp.bfloat16), vals[slot], preferred_element_type=jnp.float32)
-            if first and index == 0:
+            if index == 0:
                 acc[qs, :] = pv
+            elif index + 1 < len(blocks) or first:
+                acc[qs, :] = acc[qs, :] + pv
             else:
-                acc[qs, :] = acc[qs, :] + pv
+                if i == 0:
+                    ca.wait()
+                acc[qs, :] = acc[qs, :] + pv + old[qs, :]
+            if index == 0 and len(blocks) == 1 and not first:
+                if i == 0:
+                    ca.wait()
+                acc[qs, :] = acc[qs, :] + old[qs, :]
             if index + 1 == len(blocks):
                 if last:
                     for t in range(QB // 128):
@@ -139,12 +149,12 @@
         in_specs=specs, out_specs=ospecs, out_shape=outs,
         scratch_shapes=[
             pltpu.VMEM((n, rows, half), jnp.bfloat16), pltpu.VMEM((n, rows, half), jnp.bfloat16),
-            pltpu.VMEM((n, WROWS, half), jnp.bfloat16), pltpu.VMEM((2, KB, 2 * half), jnp.bfloat16),
+            pltpu.VMEM((n, WROWS, 128), jnp.bfloat16), pltpu.VMEM((2, KB, 2 * half), jnp.bfloat16),
             pltpu.VMEM((2, KB, wide), jnp.bfloat16),
-            pltpu.VMEM((rows, 2 * half), jnp.bfloat16), pltpu.VMEM((rows, wide), jnp.float32),
+            pltpu.VMEM((rows, 2 * half), jnp.bfloat16), pltpu.VMEM((rows, wide), jnp.float32), pltpu.VMEM((8 if first else rows, wide), jnp.float32),
             pltpu.SemaphoreType.DMA((n, 4)), pltpu.SemaphoreType.DMA, pltpu.SemaphoreType.DMA, pltpu.SemaphoreType.DMA((rows // QB,)),
         ],
-        compiler_params=pltpu.CompilerParams(vmem_limit_bytes=48 * 1024 * 1024),
+        compiler_params=pltpu.CompilerParams(vmem_limit_bytes=28 * 1024 * 1024),
         name=name,
     )(*ops)
 
@@ -173,41 +183,44 @@
     wraps = lambda step: ((slab + step * sign) % count // RING != slab // RING).astype(jnp.int32)
     flips = jnp.stack([wraps(2), wraps(-2)])
 
-    packed = jnp.full((WROWS, half), 1.0, jnp.bfloat16).at[:8, :128].set(weights.reshape(8, 128))
+    lines = weights.reshape(rows // 128, 128)
+    own_w = jnp.concatenate([lines] * (WROWS * 128 // rows), axis=0)
     inner0 = over(embeddings, inner)
     outer0 = over(embeddings, outer)
+    other = trade(embeddings)
+    inner_w = over(own_w, inner)
+    outer_w = over(own_w, outer)
+    other, inner0, outer0, inner_w, outer_w = lax.optimization_barrier(
+        (other, inner0, outer0, inner_w, outer_w)
+    )
+
+    inner1 = over(other, inner)
+    swapped1 = swap(other)
     swapped0 = swap(embeddings)
-    other = trade(jnp.concatenate([packed, embeddings], axis=0))
-    other, inner0, outer0, swapped0 = lax.optimization_barrier((other, inner0, outer0, swapped0))
-
-    cut = rows // 2
-    swapped1 = swap(other)
-    inner1 = over(other, inner)
+    swapped_w = swap(own_w)
     mate0 = swap(inner0)
-    outer1_back = trade(outer0[:cut])
-    outer1_front = over(jnp.concatenate([other[:WROWS], other[WROWS + cut :]], axis=0), outer)
-
-    whole = lambda first: {"d0": first, "d1": [(first + 1, WROWS, 0, rows)], "w": first + 1}
+    mate_w = swap(inner_w)
+    outer1 = trade(outer0)
+
+    whole = lambda first: {"d0": first, "d1": [(first + 1, 0, 0, rows)], "w": first + 2}
     queries, acc = slabs_call(
-        flips, [embeddings, other, swapped0, swapped1], [whole(0), whole(2)], [None, None], rows, half, name="own_pair"
-    )
-    acc, inner1, outer1_back, outer1_front = lax.optimization_barrier((acc, inner1, outer1_back, outer1_front))
+        flips, [embeddings, other, own_w, swapped0, swapped1, swapped_w],
+        [whole(0), whole(3)], [None, None], rows, half, name="own_pair"
+    )
+    acc, inner1, outer1 = lax.optimization_barrier((acc, inner1, outer1))
     mate1 = swap(inner1)
-    (acc,) = slabs_call(
-        flips, [inner0, inner1], [whole(0)], [0], rows, half, queries=queries, acc=acc, name="inner_slab"
-    )
-    halves = {"d0": 2, "d1": [(3, 0, 0, cut), (4, WROWS, cut, rows - cut)], "w": 4}
+    outer_slab = {"d0": 6, "d1": [(7, 0, 0, rows)], "w": 8}
     neighbours, scores = slabs_call(
         flips,
-        [mate0, mate1, outer0, outer1_back, outer1_front],
-        [whole(0), halves],
-        [1, 1],
+        [inner0, inner1, inner_w, mate0, mate1, mate_w, outer0, outer1, outer_w],
+        [whole(0), whole(3), outer_slab],
+        [0, 1, 1],
         rows,
         half,
         queries=queries,
         acc=acc,
         last=True,
-        name="last_pair",
+        name="last_three",
     )
     return neighbours, scores.reshape(rows)
 

time: 72.3 us -> 66.1 us (0.914)
  starting transfers between devices: 25.2 us -> 36.5 us
  waiting for transfers between devices: 15.2 us -> 4.69 us
  local copies, waits for them, and re-layouts: 4.2 us -> 1.13 us
  Pallas kernels: 24.5 us -> 21.9 us
  other arithmetic: 2.13 us -> 0.83 us
    ppermute x4 -> x5, waiting for transfers between devices: 15 us -> 2.02 us  [shards(): over = lambda value, pairs: lax.ppermute(value, ('blk', 'rep'), pairs)]
    ppermute x4 -> x6, starting transfers between devices: 6.56 us -> 17.7 us  [shards(): lax.ppermute(value, 'blk', [(s, s ^ 1) for s in range(count)])]
    ppermute x4 -> x6, waiting for transfers between devices: 0.01 us -> 2.67 us  [shards(): lax.ppermute(value, 'blk', [(s, s ^ 1) for s in range(count)])]
    pallas_call x3 -> x2, Pallas kernels: 24.5 us -> 21.9 us  [slabs_call(): pl.pallas_call(functools.partial(slab_kernel, sources=sources, first=firs...]
    unnamed x12 -> x2, local copies, waits for them, and re-layouts: 3.36 us -> 1.13 us
    concatenate x2 -> x1, other arithmetic: 2.05 us -> 0.76 us  [shards(): own_w = jnp.concatenate([lines] * (WROWS * 128 // rows), axis=0)]
    slice x3 -> x0, local copies, waits for them, and re-layouts: 0.83 us -> none  [the longest x1 0.79 us: shards(): outer1_back = trade(outer0[:cut])]
    ppermute x4 -> x5, starting transfers between devices: 16.4 us -> 16.3 us  [shards(): over = lambda value, pairs: lax.ppermute(value, ('blk', 'rep'), pairs)]
  transfers between devices with their start and end apart: 10 -> 13, of which waited for: 3 -> 3; matrix products, arithmetic and copies ran while one was open for 2% -> 1% of each run, Pallas kernels for 21% -> 14%
where the time goes in v3:
time: 66.1 us; the launch traced here: 66 us
  starting transfers between devices  36.5 us (55%)
  Pallas kernels  21.9 us (33%)
  waiting for transfers between devices  4.69 us (7%)
  local copies, waits for them, and re-layouts  1.13 us (2%)
  between operations  0.86 us (1%)
  other arithmetic  0.83 us (1%)
    pallas_call x2, Pallas kernels, slabs_call(): pl.pallas_call(functools.partial(slab_kernel, sources=sources, first=firs...  21.9 us
    ppermute x6, starting transfers between devices, shards(): lax.ppermute(value, 'blk', [(s, s ^ 1) for s in range(count)])  17.7 us
    ppermute x5, starting transfers between devices, shards(): over = lambda value, pairs: lax.ppermute(value, ('blk', 'rep'), pairs)  16.3 us
    ppermute x6, waiting for transfers between devices, shards(): lax.ppermute(value, 'blk', [(s, s ^ 1) for s in range(count)])  2.67 us
    ppermute x2, starting transfers between devices, shards(): trade = lambda value: lax.ppermute(value, 'rep', [(0, 1), (1, 0)])  2.53 us
    ppermute x5, waiting for transfers between devices, shards(): over = lambda value, pairs: lax.ppermute(value, ('blk', 'rep'), pairs)  2.02 us
  transfers between devices with their start and end apart: 13, of which 3 were waited for; matrix products, arithmetic and copies ran while one was open for 1% of the time, Pallas kernels for 14%

profile of v3, /device:TPU:1, one launch (start us, length us, event | category | flops | bytes accessed | tf_op | source)
XLA Modules:
  0.0 66.0 jit_solution(6927161242355615430)
XLA Ops:
  0.6 2.2 %collective-permute-start = (bf16[1024,384]{1,0:T(8,128)(2,1)}, bf16[1024,384]{1,0:T(8,128)(2,1)}, u32[]{:S(2)}, u32[]{:S(2)}) collective-permute-start(bf16[1024,384]{1,0:T(8,128)(2,1)} %refs_1_.1), channel_id=1, source_target_pairs={{0,1},{1,0},{2,3},{3,2},{4,5},{5,4},{6,7},{7,6},{8,9},{9,8},{10,11... | collective-permute-start | bytes 2359304 | tf_op jit(solution)/shard_map/ppermute | solution.py:180
  2.8 1.6 %collective-permute-start.1 = (bf16[1024,384]{1,0:T(8,128)(2,1)}, bf16[1024,384]{1,0:T(8,128)(2,1)S(1)}, u32[]{:S(2)}, u32[]{:S(2)}) collective-permute-start(bf16[1024,384]{1,0:T(8,128)(2,1)} %refs_1_.1), channel_id=1, source_target_pairs={{4,0},{5,1},{254,3},{255,2},{8,4},{9,5},{2,6},{3,7},{12,8},{13,9},... | collective-permute-start | bytes 2359304 | tf_op jit(solution)/shard_map/ppermute | solution.py:178
  4.5 7.8 %collective-permute-start.2 = (bf16[1024,384]{1,0:T(8,128)(2,1)}, bf16[1024,384]{1,0:T(8,128)(2,1)S(1)}, u32[]{:S(2)}, u32[]{:S(2)}) collective-permute-start(bf16[1024,384]{1,0:T(8,128)(2,1)} %refs_1_.1), channel_id=1, source_target_pairs={{252,1},{253,0},{6,2},{7,3},{0,4},{1,5},{10,6},{11,7},{4,8},{5,9},... | collective-permute-start | bytes 2359304 | tf_op jit(solution)/shard_map/ppermute | solution.py:178
  12.2 0.8 %pad_maximum_fusion.refs_3_ = bf16[16,128]{1,0:T(8,128)(2,1)S(1)} fusion(bf16[8,128]{1,0:T(8,128)(2,1)} %bitcast.4), kind=kLoop, calls=%fused_computation | loop fusion | flops 8192 | bytes 6144 | tf_op jit(solution)/shard_map/concatenate | solution.py:187
  13.0 0.0 collective-permute-start.3
  13.0 6.9 %collective-permute-start.4 = (bf16[16,128]{1,0:T(8,128)(2,1)S(1)}, bf16[16,128]{1,0:T(8,128)(2,1)S(1)}, u32[]{:S(2)}, u32[]{:S(2)}) collective-permute-start(bf16[16,128]{1,0:T(8,128)(2,1)S(1)} %pad_maximum_fusion.refs_3_), channel_id=1, source_target_pairs={{252,1},{253,0},{6,2},{7,3},{0,4},{1,5},{10,6},{11,7},{4,8},{5,9},... | collective-permute-start | bytes 12296 | tf_op jit(solution)/shard_map/ppermute | solution.py:178
  19.9 2.0 %collective-permute-done.3.refs_5_ = bf16[16,128]{1,0:T(8,128)(2,1)S(1)} collective-permute-done((bf16[16,128]{1,0:T(8,128)(2,1)S(1)}, bf16[16,128]{1,0:T(8,128)(2,1)S(1)}, u32[]{:S(2)}, u32[]{:S(2)}) %collective-permute-start.3) | collective-permute-done | bytes 4128 | tf_op jit(solution)/shard_map/ppermute | solution.py:178
  21.9 8.5 %collective-permute-start.5 = (bf16[1024,384]{1,0:T(8,128)(2,1)}, bf16[1024,384]{1,0:T(8,128)(2,1)}, u32[]{:S(2)}, u32[]{:S(2)}) collective-permute-start(bf16[1024,384]{1,0:T(8,128)(2,1)} %refs_1_.1), channel_id=1, source_target_pairs={{0,2},{2,0},{4,6},{6,4},{8,10},{10,8},{12,14},{14,12},{16,18},{18,... | collective-permute-start | bytes 2359304 | tf_op jit(solution)/shard_map/ppermute | solution.py:179
  30.3 0.0 collective-permute-done.4.refs_11_
  30.4 0.0 collective-permute-done.refs_2_
  30.4 0.0 collective-permute-done.1.refs_3_
  30.4 0.0 collective-permute-done.2.refs_9_
  30.4 0.9 %collective-permute-start.6 = (bf16[1024,384]{1,0:T(8,128)(2,1)}, bf16[1024,384]{1,0:T(8,128)(2,1)}, u32[]{:S(2)}, u32[]{:S(2)}) collective-permute-start(bf16[1024,384]{1,0:T(8,128)(2,1)} %collective-permute-done.refs_2_), channel_id=1, source_target_pairs={{0,2},{2,0},{4,6},{6,4},{8,10},{10,8},{12,14},{14,12},{16,18},{18,... | collective-permute-start | bytes 2359304 | tf_op jit(solution)/shard_map/ppermute | solution.py:179
  31.2 0.0 collective-permute-start.8
  31.2 0.3 collective-permute-start.9
  31.6 7.3 %collective-permute-start.7 = (bf16[16,128]{1,0:T(8,128)(2,1)S(1)}, bf16[16,128]{1,0:T(8,128)(2,1)S(1)}, u32[]{:S(2)}, u32[]{:S(2)}) collective-permute-start(bf16[16,128]{1,0:T(8,128)(2,1)S(1)} %pad_maximum_fusion.refs_3_), channel_id=1, source_target_pairs={{0,2},{2,0},{4,6},{6,4},{8,10},{10,8},{12,14},{14,12},{16,18},{18,... | collective-permute-start | bytes 12296 | tf_op jit(solution)/shard_map/ppermute | solution.py:179
  38.8 0.1 add_convert_fusion.refs_0_
  38.9 0.7 %collective-permute-done.7.refs_6_ = bf16[16,128]{1,0:T(8,128)(2,1)S(1)} collective-permute-done((bf16[16,128]{1,0:T(8,128)(2,1)S(1)}, bf16[16,128]{1,0:T(8,128)(2,1)S(1)}, u32[]{:S(2)}, u32[]{:S(2)}) %collective-permute-start.7) | collective-permute-done | bytes 4128 | tf_op jit(solution)/shard_map/ppermute | solution.py:179
  39.6 0.3 collective-permute-start.10
  40.0 0.0 collective-permute-done.5.refs_4_
  40.0 0.0 collective-permute-done.6.refs_5_
  40.0 0.0 copy-start
  40.0 1.1 %copy-done = bf16[1024,384]{1,0:T(8,128)(2,1)S(1)} copy-done((bf16[1024,384]{1,0:T(8,128)(2,1)S(1)}, bf16[1024,384]{1,0:T(8,128)(2,1)}, u32[]{:S(2)}) %copy-start) | copy-done | bytes 786456
  41.1 9.2 %own_pair.1 = (bf16[1024,768]{1,0:T(8,128)(2,1)S(1)}, f32[1024,512]{1,0:T(8,128)S(1)}) custom-call(s32[2]{0:T(128)S(1)} %add_convert_fusion.refs_0_, bf16[1024,384]{1,0:T(8,128)(2,1)S(1)} %copy-done, bf16[1024,384]{1,0:T(8,128)(2,1)} %collective-permute-done.refs_2_, bf16[16,128]{1,0:T(8,128)(2,1)S(1)} %pad_maximum_fusion.refs_3_, ...), custom_call_target="tpu_custom_call" | custom-call | tf_op jit(solution)/shard_map/own_pair/pallas_call | solution.py:147
  50.4 0.0 collective-permute-done.8.refs_4_
  50.4 0.0 collective-permute-done.9.refs_10_
  50.4 0.8 %collective-permute-start.11 = (bf16[1024,384]{1,0:T(8,128)(2,1)S(1)}, bf16[1024,384]{1,0:T(8,128)(2,1)S(1)}, u32[]{:S(2)}, u32[]{:S(2)}) collective-permute-start(bf16[1024,384]{1,0:T(8,128)(2,1)S(1)} %collective-permute-done.8.refs_4_), channel_id=1, source_target_pairs={{0,2},{2,0},{4,6},{6,4},{8,10},{10,8},{12,14},{14,12},{16,18},{18,... | collective-permute-start | bytes 2359304 | tf_op jit(solution)/shard_map/ppermute | solution.py:179
  51.2 0.0 collective-permute-start.12
  51.2 1.9 %collective-permute-done.12.refs_8_ = bf16[16,128]{1,0:T(8,128)(2,1)S(1)} collective-permute-done((bf16[16,128]{1,0:T(8,128)(2,1)S(1)}, bf16[16,128]{1,0:T(8,128)(2,1)S(1)}, u32[]{:S(2)}, u32[]{:S(2)}) %collective-permute-start.12) | collective-permute-done | bytes 4128 | tf_op jit(solution)/shard_map/ppermute | solution.py:179
  53.1 0.0 collective-permute-done.10.refs_6_
  53.1 0.0 collective-permute-done.11.refs_7_
  53.1 12.7 %last_three.1 = (bf16[1024,384]{1,0:T(8,128)(2,1)}, f32[8,128]{1,0:T(8,128)}) custom-call(s32[2]{0:T(128)S(1)} %add_convert_fusion.refs_0_, bf16[1024,768]{1,0:T(8,128)(2,1)S(1)} %get-tuple-element.15.refs_1_, f32[1024,512]{1,0:T(8,128)S(1)} %get-tuple-element.18.refs_2_, bf16[1024,384]{1,0:T(8,128)(2,1)S(1)} %collective-permute-done.1.refs_3_, ...), custom_call_target="tpu_custom_call" | custom-call | tf_op jit(solution)/shard_map/last_three/pallas_call | solution.py:147
Async XLA Ops:
  0.6 29.7 %collective-permute-start = (bf16[1024,384]{1,0:T(8,128)(2,1)}, bf16[1024,384]{1,0:T(8,128)(2,1)}, u32[]{:S(2)}, u32[]{:S(2)}) collective-permute-start(bf16[1024,384]{1,0:T(8,128)(2,1)} %refs_1_.1), channel_id=1, source_target_pairs={{0,1},{1,0},{2,3},{3,2},{4,5},{5,4},{6,7},{7,6},{8,9},{9,8},{10,11... | collective-permute-start | bytes 2359304 | tf_op jit(solution)/shard_map/ppermute | solution.py:180
  2.8 27.5 %collective-permute-start.1 = (bf16[1024,384]{1,0:T(8,128)(2,1)}, bf16[1024,384]{1,0:T(8,128)(2,1)S(1)}, u32[]{:S(2)}, u32[]{:S(2)}) collective-permute-start(bf16[1024,384]{1,0:T(8,128)(2,1)} %refs_1_.1), channel_id=1, source_target_pairs={{4,0},{5,1},{254,3},{255,2},{8,4},{9,5},{2,6},{3,7},{12,8},{13,9},... | collective-permute-start | bytes 2359304 | tf_op jit(solution)/shard_map/ppermute | solution.py:178
  4.5 25.9 %collective-permute-start.2 = (bf16[1024,384]{1,0:T(8,128)(2,1)}, bf16[1024,384]{1,0:T(8,128)(2,1)S(1)}, u32[]{:S(2)}, u32[]{:S(2)}) collective-permute-start(bf16[1024,384]{1,0:T(8,128)(2,1)} %refs_1_.1), channel_id=1, source_target_pairs={{252,1},{253,0},{6,2},{7,3},{0,4},{1,5},{10,6},{11,7},{4,8},{5,9},... | collective-permute-start | bytes 2359304 | tf_op jit(solution)/shard_map/ppermute | solution.py:178
  13.0 8.9 %collective-permute-start.3 = (bf16[16,128]{1,0:T(8,128)(2,1)S(1)}, bf16[16,128]{1,0:T(8,128)(2,1)S(1)}, u32[]{:S(2)}, u32[]{:S(2)}) collective-permute-start(bf16[16,128]{1,0:T(8,128)(2,1)S(1)} %pad_maximum_fusion.refs_3_), channel_id=1, source_target_pairs={{4,0},{5,1},{254,3},{255,2},{8,4},{9,5},{2,6},{3,7},{12,8},{13,9},... | collective-permute-start | bytes 12296 | tf_op jit(solution)/shard_map/ppermute | solution.py:178
  13.0 17.4 %collective-permute-start.4 = (bf16[16,128]{1,0:T(8,128)(2,1)S(1)}, bf16[16,128]{1,0:T(8,128)(2,1)S(1)}, u32[]{:S(2)}, u32[]{:S(2)}) collective-permute-start(bf16[16,128]{1,0:T(8,128)(2,1)S(1)} %pad_maximum_fusion.refs_3_), channel_id=1, source_target_pairs={{252,1},{253,0},{6,2},{7,3},{0,4},{1,5},{10,6},{11,7},{4,8},{5,9},... | collective-permute-start | bytes 12296 | tf_op jit(solution)/shard_map/ppermute | solution.py:178
  21.9 18.1 %collective-permute-start.5 = (bf16[1024,384]{1,0:T(8,128)(2,1)}, bf16[1024,384]{1,0:T(8,128)(2,1)}, u32[]{:S(2)}, u32[]{:S(2)}) collective-permute-start(bf16[1024,384]{1,0:T(8,128)(2,1)} %refs_1_.1), channel_id=1, source_target_pairs={{0,2},{2,0},{4,6},{6,4},{8,10},{10,8},{12,14},{14,12},{16,18},{18,... | collective-permute-start | bytes 2359304 | tf_op jit(solution)/shard_map/ppermute | solution.py:179
  30.4 9.6 %collective-permute-start.6 = (bf16[1024,384]{1,0:T(8,128)(2,1)}, bf16[1024,384]{1,0:T(8,128)(2,1)}, u32[]{:S(2)}, u32[]{:S(2)}) collective-permute-start(bf16[1024,384]{1,0:T(8,128)(2,1)} %collective-permute-done.refs_2_), channel_id=1, source_target_pairs={{0,2},{2,0},{4,6},{6,4},{8,10},{10,8},{12,14},{14,12},{16,18},{18,... | collective-permute-start | bytes 2359304 | tf_op jit(solution)/shard_map/ppermute | solution.py:179
  31.2 19.2 %collective-permute-start.8 = (bf16[1024,384]{1,0:T(8,128)(2,1)}, bf16[1024,384]{1,0:T(8,128)(2,1)S(1)}, u32[]{:S(2)}, u32[]{:S(2)}) collective-permute-start(bf16[1024,384]{1,0:T(8,128)(2,1)} %collective-permute-done.refs_2_), channel_id=1, source_target_pairs={{4,0},{5,1},{254,3},{255,2},{8,4},{9,5},{2,6},{3,7},{12,8},{13,9},... | collective-permute-start | bytes 2359304 | tf_op jit(solution)/shard_map/ppermute | solution.py:178
  31.2 19.2 %collective-permute-start.9 = (bf16[1024,384]{1,0:T(8,128)(2,1)S(1)}, bf16[1024,384]{1,0:T(8,128)(2,1)S(1)}, u32[]{:S(2)}, u32[]{:S(2)}) collective-permute-start(bf16[1024,384]{1,0:T(8,128)(2,1)S(1)} %collective-permute-done.2.refs_9_), channel_id=1, source_target_pairs={{0,1},{1,0},{2,3},{3,2},{4,5},{5,4},{6,7},{7,6},{8,9},{9,8},{10,11... | collective-permute-start | bytes 2359304 | tf_op jit(solution)/shard_map/ppermute | solution.py:180
  31.6 8.1 %collective-permute-start.7 = (bf16[16,128]{1,0:T(8,128)(2,1)S(1)}, bf16[16,128]{1,0:T(8,128)(2,1)S(1)}, u32[]{:S(2)}, u32[]{:S(2)}) collective-permute-start(bf16[16,128]{1,0:T(8,128)(2,1)S(1)} %pad_maximum_fusion.refs_3_), channel_id=1, source_target_pairs={{0,2},{2,0},{4,6},{6,4},{8,10},{10,8},{12,14},{14,12},{16,18},{18,... | collective-permute-start | bytes 12296 | tf_op jit(solution)/shard_map/ppermute | solution.py:179
  39.6 13.5 %collective-permute-start.10 = (bf16[1024,384]{1,0:T(8,128)(2,1)S(1)}, bf16[1024,384]{1,0:T(8,128)(2,1)S(1)}, u32[]{:S(2)}, u32[]{:S(2)}) collective-permute-start(bf16[1024,384]{1,0:T(8,128)(2,1)S(1)} %collective-permute-done.1.refs_3_), channel_id=1, source_target_pairs={{0,2},{2,0},{4,6},{6,4},{8,10},{10,8},{12,14},{14,12},{16,18},{18,... | collective-permute-start | bytes 2359304 | tf_op jit(solution)/shard_map/ppermute | solution.py:179
  40.0 1.1 %copy-start = (bf16[1024,384]{1,0:T(8,128)(2,1)S(1)}, bf16[1024,384]{1,0:T(8,128)(2,1)}, u32[]{:S(2)}) copy-start(bf16[1024,384]{1,0:T(8,128)(2,1)} %refs_1_.1) | copy-start | bytes 2359300
  50.4 2.7 %collective-permute-start.11 = (bf16[1024,384]{1,0:T(8,128)(2,1)S(1)}, bf16[1024,384]{1,0:T(8,128)(2,1)S(1)}, u32[]{:S(2)}, u32[]{:S(2)}) collective-permute-start(bf16[1024,384]{1,0:T(8,128)(2,1)S(1)} %collective-permute-done.8.refs_4_), channel_id=1, source_target_pairs={{0,2},{2,0},{4,6},{6,4},{8,10},{10,8},{12,14},{14,12},{16,18},{18,... | collective-permute-start | bytes 2359304 | tf_op jit(solution)/shard_map/ppermute | solution.py:179
  51.2 1.9 %collective-permute-start.12 = (bf16[16,128]{1,0:T(8,128)(2,1)S(1)}, bf16[16,128]{1,0:T(8,128)(2,1)S(1)}, u32[]{:S(2)}, u32[]{:S(2)}) collective-permute-start(bf16[16,128]{1,0:T(8,128)(2,1)S(1)} %collective-permute-done.3.refs_5_), channel_id=1, source_target_pairs={{0,2},{2,0},{4,6},{6,4},{8,10},{10,8},{12,14},{14,12},{16,18},{18,... | collective-permute-start | bytes 12296 | tf_op jit(solution)/shard_map/ppermute | solution.py:179
